TPU v7x, 32 devices: a whole 2x2x4 slice. The times are simulated.
32 devices in a mesh: rep: 2 (over y), ctx: 4 (over z), smp: 4 (over x, core).
Axes of the slice: x: 2, y: 2, z: 4, core: 2. Of those that a mesh axis runs over, the one named last changes fastest.
Arguments:
- kv: bfloat16 [65536, 576], P(('rep', 'ctx')), parts along dimension 0
- idx_key: bfloat16 [65536, 128], P(('rep', 'ctx')), parts along dimension 0
- query: bfloat16 [16, 64, 128, 576], P(('rep', 'smp'), None, 'ctx'), parts along dimension 0
- dout: bfloat16 [16, 64, 128, 512], P(('rep', 'smp'), None, 'ctx'), parts along dimension 0, may hold values from -48 to 48
- idx_query: bfloat16 [16, 64, 64, 128], P(('rep', 'smp'), None, 'ctx'), parts along dimension 0
- idx_weight: bfloat16 [16, 64, 64], P(('rep', 'smp'), None, 'ctx'), parts along dimension 0, may hold values from 0.099609375 to 1
- blocks: int32 [16, 16], P(('rep', 'smp')), parts along dimension 0, may hold values from 0 to 511, as said below
- counts: int32 [16], P(('rep', 'smp')), parts along dimension 0, may hold values from 8 to 16, as said below
Outputs:
- d_query: bfloat16 [16, 64, 128, 576], P(('rep', 'smp'), None, 'ctx'), parts along dimension 0
- d_idx_query: bfloat16 [16, 64, 64, 128], P(('rep', 'smp'), None, 'ctx'), parts along dimension 0
- d_idx_weight: bfloat16 [16, 64, 64], P(('rep', 'smp'), None, 'ctx'), parts along dimension 0
- d_kv: bfloat16 [65536, 576], P(('rep', 'ctx', 'smp')), parts along dimension 0
- d_idx_key: bfloat16 [65536, 128], P(('rep', 'ctx', 'smp')), parts along dimension 0
There are 2 independent parts, one for each index of `rep`. A program takes and returns all parts, laid end to end along the dimension named above; each array names one. Nothing has to cross between parts.
Inputs may be any that keep to these rules, and one draw needn't show every extreme that they name: The first counts[s] entries of blocks[s] are distinct and ascending, the rest are 0. Of one sample's selected blocks at most 8 lie in one shard of 8192 prompt tokens, and for every sample some shard holds exactly 8. `counts`: sample 0 of every prompt has 16.
All inputs are finite; a program needn't handle non-finite values.
Results may differ from a plain program's by a relative error of at most 0.005.
Values may be sent and summed in bfloat16 or wider, within the bound.
No kernel may reach another device: no remote copies, remote signals or barrier semaphores. Data moves between devices by JAX's collectives and lax.ppermute only.
A program may use at most 256 MiB of HBM per device.

v0:
```python
import jax
import jax.numpy as jnp
from jax import lax
from jax.sharding import PartitionSpec as P

H = 128
BLK = 64


SCALE = 192.0 ** (-0.5)
IDX_SCALE = 128.0 ** (-0.5)
LOSS = 256.0
NEG = -1e30
UPPER_LIMIT = lax.Precision.HIGHEST


def forward_part(key_rows, ikeys, live_key, query, idx_query, idx_weight):
    sn, rn, hn, width = query.shape
    flat = query.reshape(sn, rn * hn, width)
    scores = jnp.einsum("sqd,snd->sqn", flat, key_rows, preferred_element_type=jnp.float32) * SCALE
    scores = jnp.where(live_key[:, None, :], scores, NEG)
    peak = jnp.max(scores, axis=-1, keepdims=True)
    expo = jnp.exp(scores - peak)
    probability_rows = expo / jnp.sum(expo, axis=-1, keepdims=True)
    mass = jnp.sum(probability_rows.reshape(sn, rn, hn, -1), axis=2)
    inner = (
        jnp.einsum("srgd,snd->srgn", idx_query, ikeys, preferred_element_type=jnp.float32)
        * IDX_SCALE
    )
    logit = jnp.einsum(
        "srg,srgn->srn",
        idx_weight.astype(jnp.float32),
        jnp.maximum(inner, 0.0),
        precision=UPPER_LIMIT,
    )
    return (probability_rows, inner, mass, logit)


def kl_grad(mass, logit, live_key):
    target = mass / H
    masked = jnp.where(live_key[:, None, :], logit, NEG)
    peak = jnp.max(masked, axis=-1, keepdims=True)
    expo = jnp.exp(masked - peak)
    share = expo / jnp.sum(expo, axis=-1, keepdims=True)
    return LOSS * (share - target)


def backward_part(
    key_rows, ikeys, query, dout, idx_query, idx_weight, probability_rows, inner, grad
):
    sn, rn, hn, width = query.shape
    latent_state = dout.shape[-1]
    flat = query.reshape(sn, rn * hn, width)
    flat_gradient = dout.reshape(sn, rn * hn, latent_state)
    probability_gradient = jnp.einsum(
        "vbf,vgf->vbg",
        flat_gradient,
        key_rows[:, :, :latent_state],
        preferred_element_type=jnp.float32,
    )
    delta = jnp.sum(probability_rows * probability_gradient, axis=-1, keepdims=True)
    dscore = (probability_rows * (probability_gradient - delta) * SCALE).astype(jnp.bfloat16)
    dquery = (
        jnp.einsum("sqn,snd->sqd", dscore, key_rows, preferred_element_type=jnp.float32)
        .astype(jnp.bfloat16)
        .reshape(sn, rn, hn, width)
    )
    dkeys = jnp.einsum("sqn,sqd->snd", dscore, flat, preferred_element_type=jnp.float32)
    value_gradient = jnp.einsum(
        "tjw,tjv->twv",
        probability_rows.astype(jnp.bfloat16),
        flat_gradient,
        preferred_element_type=jnp.float32,
    )
    dkeys = dkeys.at[:, :, :latent_state].add(value_gradient)
    weight = idx_weight.astype(jnp.float32)
    edge = jnp.where(
        inner > 0.0, grad[:, :, None, :] * weight[:, :, :, None] * IDX_SCALE, 0.0
    ).astype(jnp.bfloat16)
    dweight = jnp.einsum(
        "srn,srgn->srg", grad, jnp.maximum(inner, 0.0), precision=UPPER_LIMIT
    ).astype(jnp.bfloat16)
    didxq = jnp.einsum("srgn,snd->srgd", edge, ikeys, preferred_element_type=jnp.float32).astype(
        jnp.bfloat16
    )
    didxk = jnp.einsum("srgn,srgd->snd", edge, idx_query, preferred_element_type=jnp.float32)
    return (dquery, didxq, dweight, dkeys, didxk)


def slot_tables(blocks, counts, n_ctx, blocks_per_shard, slots):
    listed = blocks.shape[1]
    owner = blocks // blocks_per_shard
    live_entry = jnp.arange(listed, dtype=jnp.int32)[None, :] < counts[:, None]
    marks = (
        (owner[:, :, None] == jnp.arange(n_ctx, dtype=jnp.int32)[None, None, :])
        & live_entry[:, :, None]
    ).astype(jnp.int32)
    before = jnp.cumsum(marks, axis=1) - marks
    placing = jnp.sum(before * marks, axis=2)
    slot_index = jnp.where(live_entry, owner * slots + placing, 0)
    return (owner, placing, live_entry, slot_index)


def owned_blocks(blocks, owner, placing, live_entry, me, blocks_per_shard, slots):
    mine = live_entry & (owner == me)
    picks = mine[:, None, :] & (
        placing[:, None, :] == jnp.arange(slots, dtype=jnp.int32)[None, :, None]
    )
    return jnp.sum(jnp.where(picks, (blocks % blocks_per_shard)[:, None, :], 0), axis=2)


def compact(gathered, slot_index, width):
    sn = gathered.shape[0]
    flat = gathered.reshape(sn, -1, gathered.shape[-1])
    picked = jnp.take_along_axis(flat, slot_index[:, :, None], axis=1)
    return picked.reshape(sn, -1, width)


def spread(grads, slot_index, count):
    sn, listed = slot_index.shape
    values = grads.reshape(sn, listed, -1)
    empty = jnp.zeros((sn, count, values.shape[-1]), jnp.float32)
    rows = jnp.arange(sn, dtype=jnp.int32)[:, None]
    return empty.at[rows, slot_index].add(values)


def settle(summed, local_block, blocks_per_shard):
    marks = (
        local_block.reshape(-1)[:, None] == jnp.arange(blocks_per_shard, dtype=jnp.int32)[None, :]
    ).astype(jnp.float32)
    return jnp.einsum("kb,kx->bx", marks, summed.reshape(marks.shape[0], -1), precision=UPPER_LIMIT)


def shards(kv, idx_key, query, dout, idx_query, idx_weight, blocks, counts):
    n_ctx = lax.axis_size("ctx")
    me = lax.axis_index("ctx")
    samples, listed = blocks.shape
    ctx_dev, width = kv.shape
    ind_width = idx_key.shape[1]
    blocks_per_shard = ctx_dev // BLK
    slots = max(2, 2 * listed // n_ctx)
    owner, placing, live_entry, slot_index = slot_tables(
        blocks, counts, n_ctx, blocks_per_shard, slots
    )
    live_key = jnp.repeat(live_entry, BLK, axis=1)
    local_block = owned_blocks(blocks, owner, placing, live_entry, me, blocks_per_shard, slots)
    kv_slots = jnp.take(kv.reshape(blocks_per_shard, BLK * width), local_block, axis=0)
    ik_slots = jnp.take(idx_key.reshape(blocks_per_shard, BLK * ind_width), local_block, axis=0)
    kv_all, ik_all = (
        lax.all_gather(kv_slots[:, None], "ctx", axis=1, tiled=True),
        lax.all_gather(ik_slots[:, None], "ctx", axis=1, tiled=True),
    )
    key_rows = compact(kv_all, slot_index, width)
    ikeys = compact(ik_all, slot_index, ind_width)
    probability_rows, inner, mass, logit = forward_part(
        key_rows, ikeys, live_key, query, idx_query, idx_weight
    )
    mass_all, logit_all = lax.psum((mass, logit), "ctx")
    grad = kl_grad(mass_all, logit_all, live_key)
    d_query, d_idx_query, d_idx_weight, dkeys, didxk = backward_part(
        key_rows, ikeys, query, dout, idx_query, idx_weight, probability_rows, inner, grad
    )
    slot_kv = spread(dkeys, slot_index, n_ctx * slots).reshape(samples, n_ctx, slots, -1)
    slot_ik = spread(didxk, slot_index, n_ctx * slots).reshape(samples, n_ctx, slots, -1)
    sum_kv, sum_ik = (
        lax.psum_scatter(slot_kv, "ctx", scatter_dimension=1, tiled=True),
        lax.psum_scatter(slot_ik, "ctx", scatter_dimension=1, tiled=True),
    )
    sum_kv = sum_kv.reshape(samples, slots, -1)
    sum_ik = sum_ik.reshape(samples, slots, -1)
    dense_kv = settle(sum_kv, local_block, blocks_per_shard).reshape(ctx_dev, width)
    dense_ik = settle(sum_ik, local_block, blocks_per_shard).reshape(ctx_dev, ind_width)
    out_kv, out_ik = (
        lax.psum_scatter(
            dense_kv.astype(jnp.bfloat16), "smp", scatter_dimension=0, tiled=True
        ).astype(jnp.float32),
        lax.psum_scatter(
            dense_ik.astype(jnp.bfloat16), "smp", scatter_dimension=0, tiled=True
        ).astype(jnp.float32),
    )
    return (
        d_query,
        d_idx_query,
        d_idx_weight,
        out_kv.astype(jnp.bfloat16),
        out_ik.astype(jnp.bfloat16),
    )


def solution(mesh):
    return jax.shard_map(
        shards,
        mesh=mesh,
        in_specs=(
            P(("rep", "ctx"), None),
            P(("rep", "ctx"), None),
            P(("rep", "smp"), None, "ctx", None),
            P(("rep", "smp"), None, "ctx", None),
            P(("rep", "smp"), None, "ctx", None),
            P(("rep", "smp"), None, "ctx"),
            P(("rep", "smp"), None),
            P(("rep", "smp")),
        ),
        out_specs=(
            P(("rep", "smp"), None, "ctx", None),
            P(("rep", "smp"), None, "ctx", None),
            P(("rep", "smp"), None, "ctx"),
            P(("rep", "ctx", "smp"), None),
            P(("rep", "ctx", "smp"), None),
        ),
        check_vma=False,
    )
```

profile of v0, /device:TPU:0, one launch (start us, length us, event | category | flops | bytes accessed | tf_op | source)
XLA Modules:
  0.0 904.0 jit_solution(8857074141378627737)
XLA Ops:
  14.3 14.0 %copy.65 = bf16[8192,576]{1,0:T(8,128)(2,1)} copy(bf16[8192,576]{0,1:T(8,128)(2,1)} %param.10) | data formatting | bytes 18874368 | tf_op args[0]
  28.3 18.5 %reshape.164 = bf16[128,36864]{1,0:T(8,128)(2,1)} reshape(bf16[8192,576]{1,0:T(8,128)(2,1)} %copy.65) | data formatting | bytes 18874368 | tf_op jit(solution)/shard_map/reshape | solution.py:147
  46.8 7.2 gather_fusion
  67.7 6.5 fusion.18
  75.1 72.5 %all-gather.3.cloned.1.call-done = bf16[2,4,8,36864]{3,2,0,1:T(8,128)(2,1)} async-done(((bf16[2,1,8,36864]{3,2,0,1:T(8,128)(2,1)}), bf16[2,4,8,36864]{3,2,0,1:T(8,128)(2,1)}) %all-gather.3.cloned.1.call-update) | async-done | bytes 4718608 | tf_op jit(solution)/shard_map/all_gather | solution.py:150
  152.4 8.3 gather_fusion.2
  165.8 11.2 %fusion.25 = f32[2,1024,2048]{2,1,0:T(8,128)} fusion(bf16[2,2048,512]{2,1,0:T(8,128)(2,1)} %bitcast.122, bf16[2,1024,576]{2,1,0:T(8,128)(2,1)S(1)} %broadcast_select_fusion), kind=kOutput, calls=%fused_computation.44 | convolution fusion | flops 4294967296 | bytes 23068672 | tf_op jit(solution)/shard_map/vbf,vgf->vbg/dot_general | solution.py:55
  177.0 15.4 %fusion.70 = (f32[2,2048]{1,0:T(2,128)S(1)}, f32[2,2048,1024]{1,2,0:T(8,128)}) fusion(pred[2,1024]{1,0:T(4,128)(4,1)S(1)} %broadcast_in_dim.126, bf16[2,1024,576]{2,1,0:T(8,128)(2,1)} %copy-done.4, bf16[2,2048,576]{2,1,0:T(8,128)(2,1)} %bitcast.120), kind=kOutput, calls=%fused_computation.116 | convolution fusion | flops 4848616448 | bytes 23873536 | tf_op jit(solution)/shard_map/sub | solution.py:23
  192.4 11.8 %broadcast_divide_fusion = f32[2,2048,1024]{1,2,0:T(8,128)} fusion(f32[2,2048,1024]{1,2,0:T(8,128)} %get-tuple-element.47, f32[2,2048]{1,0:T(2,128)S(1)} %get-tuple-element.46), kind=kLoop, calls=%fused_computation.27 | loop fusion | flops 4194304 | bytes 33570816 | tf_op jit(solution)/shard_map/div | solution.py:24
  204.2 18.0 %copy.74 = f32[2,2048,1024]{2,1,0:T(8,128)} copy(f32[2,2048,1024]{1,2,0:T(8,128)} %broadcast_divide_fusion) | data formatting | bytes 33554432 | tf_op jit(solution)/shard_map/div | solution.py:24
  222.2 9.8 %bitcast_reduce_fusion = f32[2,64,1024]{2,1,0:T(8,128)} fusion(f32[2,2048,1024]{2,1,0:T(8,128)} %copy.74), kind=kLoop, calls=%fused_computation.11 | loop fusion | flops 4063232 | bytes 17301504 | tf_op jit(solution)/shard_map/reduce_sum | solution.py:25
  232.0 26.4 %fusion.21 = f32[2,1024,576]{1,2,0:T(8,128)} fusion(bf16[2,2048,576]{2,1,0:T(8,128)(2,1)} %bitcast.121, f32[2,2048,1024]{1,2,0:T(8,128)} %broadcast_divide_fusion, f32[2,1024,2048]{2,1,0:T(8,128)} %fusion.25), kind=kOutput, calls=%fused_computation.36 | convolution fusion | flops 4852814848 | bytes 42991616 | tf_op jit(solution)/shard_map/sqn,sqd->snd/dot_general | solution.py:68
  258.5 12.4 %fusion.23 = f32[2,1024,576]{1,2,0:T(8,128)} fusion(f32[2,1024,576]{1,2,0:T(8,128)} %fusion.21, bf16[2,2048,512]{2,1,0:T(8,128)(2,1)} %bitcast.123, f32[2,2048,1024]{1,2,0:T(8,128)} %broadcast_divide_fusion), kind=kOutput, calls=%fused_computation.40 | convolution fusion | flops 4300210176 | bytes 29360128 | tf_op jit(solution)/shard_map/tjw,tjv->twv/dot_general | solution.py:69
  276.6 6.4 reshape.206
  287.4 47.2 %scatter_fusion = f32[2,32,36864]{2,1,0:T(8,128)} fusion(f32[2,32,36864]{2,1,0:T(8,128)} %broadcast_in_dim.143, s32[32]{0:T(128)S(1)} %reshape.204, f32[32,36864]{1,0:T(8,128)} %reshape.206), kind=kCustom, calls=%fused_computation.4 | custom fusion | flops 1179648 | bytes 14156032 | tf_op jit(solution)/shard_map/scatter-add | solution.py:124
  342.4 10.5 %scatter_fusion.1 = f32[2,32,8192]{2,1,0:T(8,128)S(1)} fusion(f32[2,32,8192]{2,1,0:T(8,128)S(1)} %broadcast_in_dim.145, s32[32]{0:T(128)S(1)} %reshape.204, f32[32,8192]{1,0:T(8,128)} %reshape.212), kind=kCustom, calls=%fused_computation.5 | custom fusion | flops 262144 | bytes 3145984 | tf_op jit(solution)/shard_map/scatter-add | solution.py:124
  355.0 392.2 %all-reduce.7.cloned.1.call-done = (f32[2,4,8,36864]{3,2,1,0:T(8,128)}, f32[2,4,8,8192]{3,2,1,0:T(8,128)}) async-done(((f32[2,4,8,36864]{3,2,1,0:T(8,128)}, f32[2,4,8,8192]{3,2,1,0:T(8,128)}), (f32[2,4,8,36864]{3,2,1,0:T(8,128)}, f32[2,4,8,8192]{3,2,1,0:T(8,128)})) %all-reduce.7.cloned.1.call-update) | async-done | bytes 11534352
  747.1 12.1 %convolution_convert_fusion = bf16[128,36864]{1,0:T(8,128)(2,1)} fusion(f32[2,4,8,36864]{3,2,1,0:T(8,128)} %get-tuple-element.37, u32[]{:T(128)} %bitcast.31, s32[16]{0:T(128)S(1)} %eq.64), kind=kOutput, calls=%fused_computation.10 | convolution fusion | flops 910690304 | bytes 11797056 | tf_op jit(solution)/shard_map/kb,kx->bx/dot_general | solution.py:131
  759.2 18.4 %convert_element_type.52 = bf16[8192,576]{1,0:T(8,128)(2,1)} reshape(bf16[128,36864]{1,0:T(8,128)(2,1)} %convolution_convert_fusion) | data formatting | bytes 18874368 | tf_op jit(solution)/shard_map/convert_element_type | solution.py:175
  784.0 30.7 %fusion.24 = bf16[2,2048,576]{1,2,0:T(8,128)(2,1)} fusion(bf16[2,1024,576]{2,1,0:T(8,128)(2,1)} %copy-done.4, f32[2,2048,1024]{1,2,0:T(8,128)} %broadcast_divide_fusion, f32[2,1024,2048]{2,1,0:T(8,128)} %fusion.25), kind=kOutput, calls=%fused_computation.41 | convolution fusion | flops 4855174144 | bytes 40632320 | tf_op jit(solution)/shard_map/sqn,snd->sqd/dot_general | solution.py:64
  814.7 7.8 copy.71
  828.1 17.3 %fusion.16 = bf16[2,64,1,16]{3,2,1,0:T(2,128)(2,1)S(1)} fusion(f32[2,64,16,1024]{3,1,2,0:T(8,128)} %copy-done.2, f32[2,64,1024,1]{2,1,0,3:T(8,128)S(1)} %bitcast.117), kind=kOutput, calls=%fused_computation.31 | convolution fusion | flops 25165824 | bytes 8916992 | tf_op jit(solution)/shard_map/srn,srgn->srg/dot_general | solution.py:80
  846.1 16.0 %reduce-scatter.5.cloned.1.call-done = bf16[2048,576]{1,0:T(8,128)(2,1)} async-done(((bf16[8192,576]{1,0:T(8,128)(2,1)}), bf16[2048,576]{1,0:T(8,128)(2,1)}) %reduce-scatter.5.cloned.1.call-update) | async-done | bytes 2359312 | tf_op jit(solution)/shard_map/reduce_scatter | solution.py:174
  866.4 30.3 %reduce-scatter.7.cloned.1.call-done = bf16[2048,128]{1,0:T(8,128)(2,1)} async-done(((bf16[8192,128]{1,0:T(8,128)(2,1)}), bf16[2048,128]{1,0:T(8,128)(2,1)}) %reduce-scatter.7.cloned.1.call-update) | async-done | bytes 524304 | tf_op jit(solution)/shard_map/reduce_scatter | solution.py:177
  (86 shorter events, 68.3 us)
Async XLA Ops:
  7.2 52.6 %copy-start = (bf16[2,64,16,128]{3,2,1,0:T(8,128)(2,1)S(1)}, bf16[2,64,16,128]{3,2,1,0:T(8,128)(2,1)}, u32[]{:S(2)}) copy-start(bf16[2,64,16,128]{3,2,1,0:T(8,128)(2,1)} %param.14) | copy-start | bytes 1572868
  7.2 48.8 %all-gather.5.cloned.1.call-start = ((), (), s32[]{:S(2)}) async-start(), calls=%async_computation.3 | async-start | bytes 1310720 | tf_op jit(solution)/shard_map/all_gather | solution.py:151
  9.2 0.6 copy-start.8
  14.2 133.4 %all-gather.3.cloned.1.call-start = ((), (), s32[]{:S(2)}) async-start(), calls=%async_computation.2 | async-start | bytes 5898240 | tf_op jit(solution)/shard_map/all_gather | solution.py:150
  46.8 8.5 copy-start.10
  46.8 9.0 copy-start.7
  55.2 279.3 %all-reduce.9.cloned.1.call-start = ((), (), s32[]{:S(2)}) async-start(), calls=%async_computation.7 | async-start | bytes 2097152 | tf_op jit(solution)/shard_map/psum | solution.py:158
  59.7 4.0 copy-start.5
  61.7 12.6 %copy-start.3 = (f32[2,1024,64,16]{1,2,3,0:T(8,128)}, f32[2,1024,64,16]{1,2,3,0:T(8,128)S(1)}, u32[]{:S(2)}) copy-start(f32[2,1024,64,16]{1,2,3,0:T(8,128)S(1)} %fusion.35) | copy-start | bytes 25165828
  63.7 4.0 copy-start.2
  165.8 11.2 %copy-start.4 = (bf16[2,1024,576]{2,1,0:T(8,128)(2,1)}, bf16[2,1024,576]{2,1,0:T(8,128)(2,1)S(1)}, u32[]{:S(2)}) copy-start(bf16[2,1024,576]{2,1,0:T(8,128)(2,1)S(1)} %broadcast_select_fusion) | copy-start | bytes 7077892
  258.4 488.7 %all-reduce.7.cloned.1.call-start = ((), (), s32[]{:S(2)}) async-start(), calls=%async_computation.6 | async-start | bytes 23068672
  352.9 1.3 copy-start.1
  352.9 1.4 copy-start.9
  352.9 1.5 copy-start.11
  354.2 507.9 %reduce-scatter.5.cloned.1.call-start = ((), (), s32[]{:S(2)}) async-start(), calls=%async_computation.4 | async-start | bytes 13107200 | tf_op jit(solution)/shard_map/reduce_scatter | solution.py:174
  777.7 119.0 %reduce-scatter.7.cloned.1.call-start = ((), (), s32[]{:S(2)}) async-start(), calls=%async_computation.5 | async-start | bytes 2621440 | tf_op jit(solution)/shard_map/reduce_scatter | solution.py:177
  814.7 7.8 copy-start.6
Sparse Core Ops, SparseCore 0:
  14.3 30.6 all-gather.4
  55.4 92.1 all-gather.2
  258.5 50.6 all-reduce.8
  354.4 392.7 all-reduce.6
  777.8 84.2 reduce-scatter.4
  865.2 31.4 reduce-scatter.6
where the time goes:
time: 912 us; the launch traced here: 904 us
  waiting for transfers between devices  511 us (56%)
  matrix products  147 us (16%)
  local copies, waits for them, and re-layouts  143 us (16%)
  other arithmetic  87.4 us (10%)
  between operations  14.9 us (2%)
    unnamed x7, waiting for transfers between devices  392 us
    all_gather x1, waiting for transfers between devices, shards(): lax.all_gather(kv_slots[:, None], 'ctx', axis=1, tiled=True)  72.5 us
    scatter-add x2, other arithmetic, spread(): return empty.at[rows, slot_index].add(values)  57.7 us
    dot_general x1, matrix products, backward_part(): jnp.einsum('sqn,snd->sqd', dscore, key_rows, preferred_element_type=jnp.f...  30.7 us
    reduce_scatter x1, waiting for transfers between devices, shards(): lax.psum_scatter(dense_ik.astype(jnp.bfloat16), 'smp', scatter_dimension=...  30.3 us
    dot_general x1, matrix products, backward_part(): jnp.einsum('sqn,sqd->snd', dscore, flat, preferred_element_type=jnp.float32)  26.4 us
    unnamed x29, local copies, waits for them, and re-layouts  26 us
    reshape x1, local copies, waits for them, and re-layouts, shards(): kv.reshape(blocks_per_shard, BLK * width)  18.5 us
  transfers between devices with their start and end apart: 6, of which 4 were waited for; matrix products, arithmetic and copies ran while one was open for 23% of the time, Pallas kernels for 0%

commit v1 on v0

v1 whole, which is shorter than its diff:
```python
import functools

import jax
import jax.numpy as jnp
from jax import lax
from jax.experimental import pallas as pl
from jax.experimental.pallas import tpu as pltpu
from jax.sharding import PartitionSpec as P

H = 128
BLK = 64
HALF = BLK // 2
LANE = 128

SCALE = 192.0 ** (-0.5)
IDX_SCALE = 128.0 ** (-0.5)
LOSS = 256.0
NEG = -1e30
EXACT = lax.Precision.HIGHEST
VMEM_BYTES = 56 * 1024 * 1024

NT = (((1,), (1,)), ((), ()))
F32 = jnp.float32
BF16 = jnp.bfloat16


def params():
    return pltpu.CompilerParams(vmem_limit_bytes=VMEM_BYTES)


def cost(flops, moved):
    return pl.CostEstimate(flops=int(flops), bytes_accessed=int(moved), transcendentals=0)


def any_spec():
    return pl.BlockSpec(memory_space=pl.ANY)


def vmem_spec():
    return pl.BlockSpec(memory_space=pltpu.VMEM)


def smem_spec():
    return pl.BlockSpec(memory_space=pltpu.SMEM)


def below(meta, base, listed, number, bound):
    total = jnp.int32(0)
    for i in range(listed):
        total += jnp.where((i < number) & (meta[base + i] < bound), 1, 0)
    return total


def span(meta, base, listed, number, shard, per_shard):
    first = below(meta, base, listed, number, shard * per_shard)
    last = below(meta, base, listed, number, (shard + 1) * per_shard)
    return first, last - first


def pack_kernel(dims, meta, kv, ik, *rest):
    samples, listed, slots, per_shard, width, tiles = dims
    outs, (kbuf, ibuf, sem) = rest[:samples], rest[samples:]
    me = meta[samples * (listed + 1)]
    copies = []
    for s in range(samples):
        number = meta[samples * listed + s]
        first, _ = span(meta, s * listed, listed, number, me, per_shard)
        for j in range(slots):
            place = jnp.minimum(first + j, listed - 1)
            block = jnp.clip(meta[s * listed + place] - me * per_shard, 0, per_shard - 1)
            rows = pl.ds(pl.multiple_of(block * BLK, BLK), BLK)
            at = s * slots + j
            one = pltpu.make_async_copy(kv.at[rows], kbuf.at[at], sem.at[at, 0])
            two = pltpu.make_async_copy(ik.at[rows], ibuf.at[at], sem.at[at, 1])
            one.start()
            two.start()
            copies.append((one, two))
    for s in range(samples):
        for j in range(slots):
            at = s * slots + j
            copies[at][0].wait()
            copies[at][1].wait()
            out = outs[s]
            for c in range(tiles):
                out[pl.ds((c * slots + j) * BLK, BLK), :] = kbuf[at, :, c * LANE : (c + 1) * LANE]
            out[pl.ds((tiles * slots + j) * BLK, BLK), :] = ibuf[at]
            tail = kbuf[at, :, tiles * LANE : width]
            out[pl.ds((tiles + 1) * slots * BLK + j * HALF, HALF), :] = jnp.concatenate(
                [tail[:HALF], tail[HALF:]], axis=1
            )


def pack(meta, kv, ik, dims):
    samples, listed, slots, per_shard, width, tiles = dims
    rows = slots * ((tiles + 1) * BLK + HALF)
    return pl.pallas_call(
        functools.partial(pack_kernel, dims),
        out_shape=[jax.ShapeDtypeStruct((rows, LANE), BF16)] * samples,
        in_specs=[smem_spec(), any_spec(), any_spec()],
        out_specs=[vmem_spec()] * samples,
        scratch_shapes=[
            pltpu.VMEM((samples * slots, BLK, width), BF16),
            pltpu.VMEM((samples * slots, BLK, ik.shape[1]), BF16),
            pltpu.SemaphoreType.DMA((samples * slots, 2)),
        ],
        compiler_params=params(),
        cost_estimate=cost(0, 4 * samples * rows * LANE * 2),
        name="pack",
    )(meta, kv, ik)


def attention_kernel(dims, s, n_ctx, heads, groups, tall, aliased, meta, *refs):
    samples, listed, slots, per_shard, width, tiles = dims
    near = 2 * n_ctx - 1
    q_ref, do_ref, iq_ref, wcol_ref = refs[:4]
    slabs = refs[4 : 4 + near]
    refs = refs[4 + near + (1 if aliased else 0) :]
    dq_ref, ikey_ref = refs[:2]
    outs = refs[2 : 2 + near]
    parts = refs[2 + near : 2 + near + n_ctx]
    k_scr, kt_scr, acc, mass_t, logits, shares = refs[2 + near + n_ctx :]
    step = pl.program_id(0)
    steps = pl.num_programs(0)
    value = tiles * LANE
    keys = listed * BLK
    rows = q_ref.shape[0]
    times = rows // heads
    me = meta[samples * (listed + 1)]
    number = meta[samples * listed + s]
    live = number * BLK

    def shard_of(at):
        if at == 0:
            return me
        return me - at if at < n_ctx else me + (at - n_ctx + 1)

    @pl.when(step == 0)
    def _():
        for at in range(near):
            slab = slabs[at]
            first, many = span(meta, s * listed, listed, number, shard_of(at), per_shard)

            def place(j, _, slab=slab, first=first):
                to = pl.multiple_of((first + j) * BLK, BLK)
                for c in range(tiles + 1):
                    piece = slab[pl.ds(pl.multiple_of((c * slots + j) * BLK, BLK), BLK), :]
                    if c < tiles:
                        k_scr[pl.ds(to, BLK), c * LANE : (c + 1) * LANE] = piece
                    else:
                        ikey_ref[pl.ds(to, BLK), :] = piece
                piece = slab[
                    pl.ds(pl.multiple_of((tiles + 1) * slots * BLK + j * HALF, HALF), HALF), :
                ]
                side = LANE // 2
                k_scr[pl.ds(to, HALF), value : value + side] = piece[:, :side]
                k_scr[pl.ds(pl.multiple_of(to + HALF, HALF), HALF), value : value + side] = piece[
                    :, side:
                ]
                return 0

            lax.fori_loop(0, many, place, 0)

        def clear(i, _):
            to = pl.multiple_of(i * BLK, BLK)
            k_scr[pl.ds(to, BLK), :] = jnp.zeros((BLK, k_scr.shape[1]), BF16)
            ikey_ref[pl.ds(to, BLK), :] = jnp.zeros((BLK, ikey_ref.shape[1]), BF16)
            return 0

        lax.fori_loop(number, listed, clear, 0)
        k_scr[:, width:] = jnp.zeros((keys, k_scr.shape[1] - width), BF16)
        kt_scr[...] = k_scr[...].T
        acc[...] = jnp.zeros_like(acc)
        mass_t[...] = jnp.zeros_like(mass_t)

    q = q_ref[...]
    do = do_ref[...]
    scores = lax.dot_general(k_scr[:, :width], q, NT, preferred_element_type=F32)
    alive = lax.broadcasted_iota(jnp.int32, (keys, 1), 0) < live
    scores = jnp.where(alive, scores * SCALE, NEG)
    expo = jnp.exp(scores - jnp.max(scores, axis=0, keepdims=True))
    probs = expo * (1.0 / jnp.sum(expo, axis=0, keepdims=True))
    probs_b = probs.astype(BF16)
    dprob = lax.dot_general(k_scr[:, :value], do, NT, preferred_element_type=F32)
    delta = jnp.sum(probs * dprob, axis=0, keepdims=True)
    dscore = (probs * (dprob - delta) * SCALE).astype(BF16)
    dq_t = jnp.dot(kt_scr[...], dscore, preferred_element_type=F32)
    dq_ref[...] = dq_t.T[:, :width].astype(BF16)
    acc[:, :width] += jnp.dot(dscore, q, preferred_element_type=F32)
    acc[:, :value] += jnp.dot(probs_b, do, preferred_element_type=F32)
    every = mass_t.shape[1]
    row = lax.broadcasted_iota(jnp.int32, (rows, every), 0) // heads + step * times
    column = lax.broadcasted_iota(jnp.int32, (rows, every), 1)
    member = jnp.where(row == column, 1.0, 0.0).astype(BF16)
    mass_t[...] += jnp.dot(probs_b, member, preferred_element_type=F32)

    inner = lax.dot_general(iq_ref[...], ikey_ref[...], NT, preferred_element_type=F32)
    weighed = jnp.maximum(inner, 0.0) * (wcol_ref[...] * IDX_SCALE)
    if groups % 8 == 0:
        logit = jnp.sum(weighed.reshape(times, groups, keys), axis=1)
    else:
        gather = (
            lax.broadcasted_iota(jnp.int32, (times, times * groups), 1) // groups
            == lax.broadcasted_iota(jnp.int32, (times, times * groups), 0)
        ).astype(F32)
        logit = jnp.dot(gather, weighed, precision=EXACT, preferred_element_type=F32)
    logits[pl.ds(pl.multiple_of(step * times, times), times), :] = logit

    @pl.when(step == steps - 1)
    def _():
        for at in range(near):
            out = outs[at]
            first, many = span(meta, s * listed, listed, number, shard_of(at), per_shard)

            def emit(j, _, out=out, first=first):
                rows = pl.ds(pl.multiple_of((first + j) * BLK, BLK), BLK)
                for c in range(tiles):
                    out[pl.ds(pl.multiple_of((c * slots + j) * BLK, BLK), BLK), :] = acc[
                        rows, c * LANE : (c + 1) * LANE
                    ].astype(BF16)
                tail = acc[rows, value : value + LANE // 2].astype(BF16)
                out[pl.ds(pl.multiple_of(tiles * slots * BLK + j * HALF, HALF), HALF), :] = (
                    jnp.concatenate([tail[:HALF], tail[HALF:]], axis=1)
                )
                return 0

            lax.fori_loop(0, many, emit, 0)
        mass = mass_t[...].T
        part = every // n_ctx
        for c in range(n_ctx):
            shares[c, :part] = mass[c * part : (c + 1) * part]
            shares[c, part:] = logits[c * part : (c + 1) * part, :]
        for k in range(n_ctx):
            parts[k][...] = shares[lax.rem(me + k, n_ctx)]


def attention(meta, query, dout, idx_query, wcol, slabs, d_query, dims, s, n_ctx, heads, tall):
    samples, listed, slots, per_shard, width, tiles = dims
    total = query.shape[1]
    every = total // heads
    groups = idx_query.shape[1] // every
    side = tall // heads * groups
    steps = total // tall
    value = tiles * LANE
    keys = listed * BLK
    wide = (width + LANE - 1) // LANE * LANE
    near = 2 * n_ctx - 1
    ind = idx_query.shape[2]
    aliased = d_query is not None
    grad_rows = slots * (tiles * BLK + HALF)
    part = every // n_ctx

    def row_spec(size, columns):
        return pl.BlockSpec((None, size, columns), lambda i: (s, i, 0))

    def whole(shape):
        return pl.BlockSpec(shape, lambda i: (0,) * len(shape))

    in_specs = [
        smem_spec(),
        row_spec(tall, width),
        row_spec(tall, value),
        row_spec(side, ind),
        row_spec(side, 1),
    ] + [whole(slabs[0].shape)] * near
    args = [meta, query, dout, idx_query, wcol] + slabs
    aliases = {}
    if aliased:
        in_specs.append(any_spec())
        aliases = {len(args): 0}
        args.append(d_query)
    out_shape = (
        [
            jax.ShapeDtypeStruct(query.shape, BF16),
            jax.ShapeDtypeStruct((keys, ind), BF16),
        ]
        + [jax.ShapeDtypeStruct((grad_rows, LANE), BF16)] * near
        + [jax.ShapeDtypeStruct((2 * part, keys), F32)] * n_ctx
    )
    out_specs = (
        [row_spec(tall, width), whole((keys, ind))]
        + [whole((grad_rows, LANE))] * near
        + [whole((2 * part, keys))] * n_ctx
    )
    flops = 2 * total * keys * (3 * width + 2 * value) + 2 * total // heads * groups * keys * ind
    out = pl.pallas_call(
        functools.partial(attention_kernel, dims, s, n_ctx, heads, groups, tall, aliased),
        grid=(steps,),
        out_shape=out_shape,
        in_specs=in_specs,
        out_specs=out_specs,
        scratch_shapes=[
            pltpu.VMEM((keys, wide), BF16),
            pltpu.VMEM((wide, keys), BF16),
            pltpu.VMEM((keys, wide), F32),
            pltpu.VMEM((keys, every), F32),
            pltpu.VMEM((every, keys), F32),
            pltpu.VMEM((n_ctx, 2 * part, keys), F32),
        ],
        input_output_aliases=aliases,
        compiler_params=params(),
        cost_estimate=cost(flops, total * (2 * width + value) * 2 + 14 * grad_rows * LANE * 2),
        name="attention",
    )(*args)
    return out[0], out[1], out[2 : 2 + near], out[2 + near :]


def divergence_kernel(samples, listed, n_ctx, meta, *refs):
    out = refs[-1]
    part, keys = out.shape[1:]
    for s in range(samples):
        total = refs[s * n_ctx][...]
        for k in range(1, n_ctx):
            total += refs[s * n_ctx + k][...]
        live = meta[samples * listed + s] * BLK
        alive = lax.broadcasted_iota(jnp.int32, (1, keys), 1) < live
        logit = jnp.where(alive, total[part:], NEG)
        expo = jnp.exp(logit - jnp.max(logit, axis=1, keepdims=True))
        share = expo / jnp.sum(expo, axis=1, keepdims=True)
        out[s] = LOSS * (share - total[:part] * (1.0 / H))


def divergence(meta, pieces, samples, listed, n_ctx):
    both, keys = pieces[0].shape
    return pl.pallas_call(
        functools.partial(divergence_kernel, samples, listed, n_ctx),
        out_shape=jax.ShapeDtypeStruct((samples, both // 2, keys), F32),
        in_specs=[smem_spec()] + [vmem_spec()] * len(pieces),
        out_specs=vmem_spec(),
        compiler_params=params(),
        cost_estimate=cost(0, len(pieces) * both * keys * 4),
        name="divergence",
    )(meta, *pieces)


def indexer_kernel(dims, n_ctx, groups, meta, *refs):
    samples, listed, slots, per_shard, width, tiles = dims
    near = 2 * n_ctx - 1
    iq_ref, wcol_ref = refs[:2]
    ikeys = refs[2 : 2 + samples]
    grads = refs[2 + samples : 2 + samples + n_ctx]
    refs = refs[2 + samples + n_ctx :]
    diq_ref, dw_ref = refs[:2]
    outs = refs[2 : 2 + near]
    whole, ik_scr, acc_t, acc = refs[2 + near :]
    s, c = pl.program_id(0), pl.program_id(1)
    me = meta[samples * (listed + 1)]
    part, keys = grads[0].shape[1:]

    @pl.when(c == 0)
    def _():
        for k in range(n_ctx):
            whole[lax.rem(me - k + n_ctx, n_ctx)] = grads[k][s]
        for at in range(samples):

            @pl.when(s == at)
            def _(at=at):
                ik_scr[...] = ikeys[at][...]

        acc_t[...] = jnp.zeros_like(acc_t)

    iq = iq_ref[...]
    inner = lax.dot_general(iq, ik_scr[...], NT, preferred_element_type=F32)
    grad = whole[c]
    if groups % 8 == 0:
        grad = jnp.broadcast_to(grad[:, None, :], (part, groups, keys)).reshape(part * groups, keys)
    else:
        expand = (
            lax.broadcasted_iota(jnp.int32, (part * groups, part), 0) // groups
            == lax.broadcasted_iota(jnp.int32, (part * groups, part), 1)
        ).astype(F32)
        grad = jnp.dot(expand, grad, precision=EXACT, preferred_element_type=F32)
    edge = jnp.where(inner > 0.0, grad * (wcol_ref[...] * IDX_SCALE), 0.0).astype(BF16)
    dw_ref[...] = jnp.sum(grad * jnp.maximum(inner, 0.0), axis=1, keepdims=True) * IDX_SCALE
    diq_ref[...] = jnp.dot(edge, ik_scr[...], preferred_element_type=F32).astype(BF16)
    acc_t[...] += jnp.dot(iq.T, edge, preferred_element_type=F32)

    @pl.when(c == n_ctx - 1)
    def _():
        acc[...] = acc_t[...].T.astype(BF16)
        number = meta[samples * listed + s]
        for at in range(near):
            shard = me if at == 0 else (me - at if at < n_ctx else me + (at - n_ctx + 1))
            first, many = span(meta, s * listed, listed, number, shard, per_shard)

            def emit(j, _, out=outs[at], first=first):
                out[pl.ds(pl.multiple_of(j * BLK, BLK), BLK), :] = acc[
                    pl.ds(pl.multiple_of((first + j) * BLK, BLK), BLK), :
                ]
                return 0

            lax.fori_loop(0, many, emit, 0)


def indexer(meta, idx_query, wcol, ikeys, grads, dims, n_ctx):
    samples, listed, slots, per_shard, width, tiles = dims
    total, ind = idx_query.shape[1:]
    part, keys = grads[0].shape[1:]
    groups = total // (part * n_ctx)
    near = 2 * n_ctx - 1
    chunk = part * groups

    def rows(columns):
        return pl.BlockSpec((None, chunk, columns), lambda s, c: (s, c, 0))

    def whole(shape):
        return pl.BlockSpec(shape, lambda s, c: (0,) * len(shape))

    slot_rows = slots * BLK
    out = pl.pallas_call(
        functools.partial(indexer_kernel, dims, n_ctx, groups),
        grid=(samples, n_ctx),
        out_shape=[
            jax.ShapeDtypeStruct(idx_query.shape, BF16),
            jax.ShapeDtypeStruct((samples, total, 1), F32),
        ]
        + [jax.ShapeDtypeStruct((samples, slot_rows, ind), BF16)] * near,
        in_specs=[smem_spec(), rows(ind), rows(1)]
        + [whole((keys, ind))] * samples
        + [whole(grads[0].shape)] * n_ctx,
        out_specs=[rows(ind), rows(1)]
        + [pl.BlockSpec((None, slot_rows, ind), lambda s, c: (s, 0, 0))] * near,
        scratch_shapes=[
            pltpu.VMEM((n_ctx, part, keys), F32),
            pltpu.VMEM((keys, ind), BF16),
            pltpu.VMEM((ind, keys), F32),
            pltpu.VMEM((keys, ind), BF16),
        ],
        compiler_params=params(),
        cost_estimate=cost(6 * samples * total * keys * ind, 8 * samples * total * LANE * 2),
        name="indexer",
    )(meta, idx_query, wcol, *ikeys, *grads)
    return out[0], out[1], out[2:]


def settle_kernel(dims, n_smp, here, *refs):
    samples, listed, slots, per_shard, width, tiles = dims
    slabs = refs[: n_smp * samples]
    iks = refs[n_smp * samples : n_smp * (samples + 1)]
    out_kv, out_ik, acc, acc_i = refs[n_smp * (samples + 1) :]
    each = samples * (listed + 1)
    me = here[n_smp * each]
    place = here[n_smp * each + 1]
    mine = per_shard // n_smp
    base = me * per_shard + place * mine
    value = tiles * LANE
    acc[...] = jnp.zeros_like(acc)
    acc_i[...] = jnp.zeros_like(acc_i)
    for at in range(n_smp):
        chips = n_smp // 2
        core, chip = at // chips, at % chips
        source = lax.rem((place ^ core) - 2 * chip + n_smp, n_smp)
        for s in range(samples):
            start = source * each + s * listed
            number = here[source * each + samples * listed + s]
            shard_first, _ = span(here, start, listed, number, me, per_shard)
            first = below(here, start, listed, number, base)
            last = below(here, start, listed, number, base + mine)

            def add(i, _, slab=slabs[at * samples + s], ik=iks[at], s=s, start=start, zero=shard_first):
                j = i - zero
                to = pl.multiple_of((here[start + i] - base) * BLK, BLK)
                rows = pl.ds(to, BLK)
                for c in range(tiles):
                    acc[rows, c * LANE : (c + 1) * LANE] += slab[
                        pl.ds(pl.multiple_of((c * slots + j) * BLK, BLK), BLK), :
                    ].astype(F32)
                tail = slab[
                    pl.ds(pl.multiple_of(tiles * slots * BLK + j * HALF, HALF), HALF), :
                ].astype(F32)
                side = LANE // 2
                acc[pl.ds(to, HALF), value : value + side] += tail[:, :side]
                acc[pl.ds(pl.multiple_of(to + HALF, HALF), HALF), value : value + side] += tail[
                    :, side:
                ]
                acc_i[rows, :] += ik[s, pl.ds(pl.multiple_of(j * BLK, BLK), BLK), :].astype(F32)
                return 0

            lax.fori_loop(first, last, add, 0)
    out_kv[...] = acc[:, :width].astype(BF16)
    out_ik[...] = acc_i[...].astype(BF16)


def settle(here, slabs, iks, dims, n_smp):
    samples, listed, slots, per_shard, width, tiles = dims
    rows = per_shard * BLK // n_smp
    ind = iks[0].shape[2]
    wide = (width + LANE - 1) // LANE * LANE
    return pl.pallas_call(
        functools.partial(settle_kernel, dims, n_smp),
        out_shape=[
            jax.ShapeDtypeStruct((rows, width), BF16),
            jax.ShapeDtypeStruct((rows, ind), BF16),
        ],
        in_specs=[smem_spec()] + [vmem_spec()] * (len(slabs) + len(iks)),
        out_specs=[vmem_spec()] * 2,
        scratch_shapes=[pltpu.VMEM((rows, wide), F32), pltpu.VMEM((rows, ind), F32)],
        compiler_params=params(),
        cost_estimate=cost(0, 4 * rows * width * 2),
        name="settle",
    )(here, *slabs, *iks)


def spread_blocks(own, n):
    rights, lefts = [], []
    right = left = own
    for step in range(1, n):
        right = lax.ppermute(right, "ctx", [(i, i + 1) for i in range(step - 1, n - 1)])
        left = lax.ppermute(left, "ctx", [(i, i - 1) for i in range(1, n - step + 1)])
        rights.append(right)
        lefts.append(left)
    return [own] + rights + lefts


def gather_sums(parts, n):
    before, after = parts[1:n], parts[n:]

    def add(a, b):
        return (a.astype(F32) + b.astype(F32)).astype(BF16)

    left, right = before[n - 2], after[n - 2]
    for far in range(n - 1, 0, -1):
        right = lax.ppermute(right, "ctx", [(i, i + 1) for i in range(n - far)])
        left = lax.ppermute(left, "ctx", [(i, i - 1) for i in range(far, n)])
        if far > 1:
            right = add(right, after[far - 2])
            left = add(left, before[far - 2])
    return (parts[0].astype(F32) + right.astype(F32) + left.astype(F32)).astype(BF16)


def shifted(x, axis, n, by):
    return lax.ppermute(x, axis, [(i, (i + by) % n) for i in range(n)])


def exchange(x, n):
    chips = [x] + [shifted(x, "smp", n, 2 * k) for k in range(1, n // 2)]
    other = [lax.ppermute(y, "smp", [(i, i ^ 1) for i in range(n)]) for y in chips]
    return chips + other


def shards(kv, idx_key, query, dout, idx_query, idx_weight, blocks, counts):
    n_ctx = lax.axis_size("ctx")
    n_smp = lax.axis_size("smp")
    me = lax.axis_index("ctx").astype(jnp.int32)
    place = lax.axis_index("smp").astype(jnp.int32)
    samples, listed = blocks.shape
    width = kv.shape[1]
    value = dout.shape[3]
    _, every, heads, _ = query.shape
    groups = idx_query.shape[2]
    dims = (
        samples,
        listed,
        max(2, 2 * listed // n_ctx),
        kv.shape[0] // BLK,
        width,
        value // LANE,
    )
    lists = jnp.concatenate([blocks.reshape(-1), counts])
    meta = jnp.concatenate([lists, me[None]])
    here = jnp.concatenate(
        [lax.all_gather(lists, "smp").reshape(-1), jnp.stack([me, place])]
    )
    q = query.reshape(samples, every * heads, width)
    do = dout.reshape(samples, every * heads, value)
    iq = idx_query.reshape(samples, every * groups, idx_query.shape[3])
    wcol = idx_weight.astype(F32).reshape(samples, every * groups, 1)
    tall = min(256, every * heads)

    slabs = [spread_blocks(own, n_ctx) for own in pack(meta, kv, idx_key, dims)]
    d_query = None
    ikeys, sums, pieces = [], [], []
    for s in range(samples):
        d_query, ikey, grads, parts = attention(
            meta, q, do, iq, wcol, slabs[s], d_query, dims, s, n_ctx, heads, tall
        )
        ikeys.append(ikey)
        pieces += [parts[0]] + [shifted(parts[k], "ctx", n_ctx, k) for k in range(1, n_ctx)]
        sums.append(gather_sums(grads, n_ctx))
    grad = divergence(meta, pieces, samples, listed, n_ctx)
    grads = [grad] + [shifted(grad, "ctx", n_ctx, k) for k in range(1, n_ctx)]
    d_idx_query, d_weight, parts = indexer(meta, iq, wcol, ikeys, grads, dims, n_ctx)
    iks = exchange(gather_sums(parts, n_ctx), n_smp)
    exchanged = [exchange(x, n_smp) for x in sums]
    out_kv, out_ik = settle(
        here, [exchanged[s][at] for at in range(n_smp) for s in range(samples)], iks, dims, n_smp
    )
    return (
        d_query.reshape(query.shape),
        d_idx_query.reshape(idx_query.shape),
        d_weight.reshape(idx_weight.shape).astype(BF16),
        out_kv,
        out_ik,
    )


def solution(mesh):
    return jax.shard_map(
        shards,
        mesh=mesh,
        in_specs=(
            P(("rep", "ctx"), None),
            P(("rep", "ctx"), None),
            P(("rep", "smp"), None, "ctx", None),
            P(("rep", "smp"), None, "ctx", None),
            P(("rep", "smp"), None, "ctx", None),
            P(("rep", "smp"), None, "ctx"),
            P(("rep", "smp"), None),
            P(("rep", "smp")),
        ),
        out_specs=(
            P(("rep", "smp"), None, "ctx", None),
            P(("rep", "smp"), None, "ctx", None),
            P(("rep", "smp"), None, "ctx"),
            P(("rep", "ctx", "smp"), None),
            P(("rep", "ctx", "smp"), None),
        ),
        check_vma=False,
    )
```

time: 912 us -> 379 us (0.42)
  waiting for transfers between devices: 511 us -> 144 us
  matrix products: 147 us -> 0 us
  local copies, waits for them, and re-layouts: 143 us -> 24.6 us
  starting transfers between devices: 0.25 us -> 106 us
  Pallas kernels: 0 us -> 88.9 us
  other arithmetic: 87.4 us -> 5.89 us
  between operations: 14.9 us -> 2.18 us
    unnamed x7 -> x0, waiting for transfers between devices: 392 us -> none
    ppermute x0 -> x48, waiting for transfers between devices: none -> 144 us  [the longest x6 58.5 us: spread_blocks(): lax.ppermute(left, 'ctx', [(i, i - 1) for i in range(1, n - step + 1)])]
    dot_general x11 -> x0, matrix products: 131 us -> none  [the longest x1 30.7 us: backward_part(): jnp.einsum('sqn,snd->sqd', dscore, key_rows, preferred_element_type=jnp.f...]
    ppermute x0 -> x48, starting transfers between devices: none -> 106 us  [the longest x12 38.9 us: shifted(): return lax.ppermute(x, axis, [(i, (i + by) % n) for i in range(n)])]
    pallas_call x0 -> x6, Pallas kernels: none -> 88.9 us  [the longest x2 66 us: attention(): pl.pallas_call(functools.partial(attention_kernel, dims, s, n_ctx, heads,...]
    all_gather x2 -> x0, waiting for transfers between devices: 72.5 us -> none  [the longest x1 72.5 us: shards(): lax.all_gather(kv_slots[:, None], 'ctx', axis=1, tiled=True)]
    scatter-add x2 -> x0, other arithmetic: 57.7 us -> none  [spread(): return empty.at[rows, slot_index].add(values)]
    reduce_scatter x2 -> x0, waiting for transfers between devices: 46.3 us -> none  [the longest x1 30.3 us: shards(): lax.psum_scatter(dense_ik.astype(jnp.bfloat16), 'smp', scatter_dimension=...]
  transfers between devices with their start and end apart: 6 -> 48, of which waited for: 4 -> 22; matrix products, arithmetic and copies ran while one was open for 23% -> 2% of each run, Pallas kernels for 0% -> 9%
where the time goes in v1:
time: 379 us; the launch traced here: 378 us
  waiting for transfers between devices  144 us (38%)
  starting transfers between devices  106 us (28%)
  Pallas kernels  88.9 us (23%)
  local copies, waits for them, and re-layouts  24.6 us (6%)
  blocking collectives  7.03 us (2%)
  other arithmetic  5.89 us (2%)
    pallas_call x2, Pallas kernels, attention(): pl.pallas_call(functools.partial(attention_kernel, dims, s, n_ctx, heads,...  66 us
    ppermute x6, waiting for transfers between devices, spread_blocks(): lax.ppermute(left, 'ctx', [(i, i - 1) for i in range(1, n - step + 1)])  58.5 us
    ppermute x12, waiting for transfers between devices, shifted(): return lax.ppermute(x, axis, [(i, (i + by) % n) for i in range(n)])  40.9 us
    ppermute x9, waiting for transfers between devices, gather_sums(): right = lax.ppermute(right, 'ctx', [(i, i + 1) for i in range(n - far)])  40.2 us
    ppermute x12, starting transfers between devices, shifted(): return lax.ppermute(x, axis, [(i, (i + by) % n) for i in range(n)])  38.9 us
    ppermute x9, starting transfers between devices, gather_sums(): right = lax.ppermute(right, 'ctx', [(i, i + 1) for i in range(n - far)])  34.8 us
    unnamed x93, local copies, waits for them, and re-layouts  22.1 us
    ppermute x6, starting transfers between devices, spread_blocks(): lax.ppermute(right, 'ctx', [(i, i + 1) for i in range(step - 1, n - 1)])  15.3 us
  transfers between devices with their start and end apart: 48, of which 22 were waited for; matrix products, arithmetic and copies ran while one was open for 2% of the time, Pallas kernels for 9%

profile of v1, /device:TPU:0, one launch (start us, length us, event | category | flops | bytes accessed | tf_op | source)
XLA Modules:
  0.0 377.8 jit_solution(16728376777680609451)
XLA Ops:
  1.4 13.9 %copy.19.kv = bf16[8192,576]{1,0:T(8,128)(2,1)} copy(bf16[8192,576]{0,1:T(8,128)(2,1)} %param.8) | data formatting | bytes 18874368 | tf_op args[0]
  22.1 5.3 %collective-permute-start.6 = (bf16[2816,128]{1,0:T(8,128)(2,1)}, bf16[2816,128]{1,0:T(8,128)(2,1)S(1)}, u32[]{:S(2)}, u32[]{:S(2)}) collective-permute-start(bf16[2816,128]{1,0:T(8,128)(2,1)} %get-tuple-element.45.refs_4_), channel_id=1, source_target_pairs={{0,4},{4,8},{8,12},{1,5},{5,9},{9,13},{2,6},{6,10},{10,14},{3,7},{... | collective-permute-start | bytes 2162696 | tf_op jit(solution)/shard_map/ppermute | solution.py:507
  33.3 9.3 %collective-permute-done.9.refs_8_ = bf16[2816,128]{1,0:T(8,128)(2,1)S(1)} collective-permute-done((bf16[2816,128]{1,0:T(8,128)(2,1)}, bf16[2816,128]{1,0:T(8,128)(2,1)S(1)}, u32[]{:S(2)}, u32[]{:S(2)}) %collective-permute-start.9) | collective-permute-done | bytes 720928 | tf_op jit(solution)/shard_map/ppermute | solution.py:508
  45.7 12.3 %collective-permute-done.3.refs_8_ = bf16[2816,128]{1,0:T(8,128)(2,1)S(1)} collective-permute-done((bf16[2816,128]{1,0:T(8,128)(2,1)}, bf16[2816,128]{1,0:T(8,128)(2,1)S(1)}, u32[]{:S(2)}, u32[]{:S(2)}) %collective-permute-start.3) | collective-permute-done | bytes 720928 | tf_op jit(solution)/shard_map/ppermute | solution.py:508
  60.8 12.7 %collective-permute-done.10.refs_9_ = bf16[2816,128]{1,0:T(8,128)(2,1)} collective-permute-done((bf16[2816,128]{1,0:T(8,128)(2,1)S(1)}, bf16[2816,128]{1,0:T(8,128)(2,1)}, u32[]{:S(2)}, u32[]{:S(2)}) %collective-permute-start.10) | collective-permute-done | bytes 720928 | tf_op jit(solution)/shard_map/ppermute | solution.py:508
  78.0 11.0 %collective-permute-done.4.refs_9_ = bf16[2816,128]{1,0:T(8,128)(2,1)} collective-permute-done((bf16[2816,128]{1,0:T(8,128)(2,1)S(1)}, bf16[2816,128]{1,0:T(8,128)(2,1)}, u32[]{:S(2)}, u32[]{:S(2)}) %collective-permute-start.4) | collective-permute-done | bytes 720928 | tf_op jit(solution)/shard_map/ppermute | solution.py:508
  91.2 13.3 %collective-permute-done.11.refs_10_ = bf16[2816,128]{1,0:T(8,128)(2,1)} collective-permute-done((bf16[2816,128]{1,0:T(8,128)(2,1)}, bf16[2816,128]{1,0:T(8,128)(2,1)}, u32[]{:S(2)}, u32[]{:S(2)}) %collective-permute-start.11) | collective-permute-done | bytes 720928 | tf_op jit(solution)/shard_map/ppermute | solution.py:508
  104.5 33.5 %attention.2 = (bf16[2,2048,576]{2,1,0:T(8,128)(2,1)}, bf16[1024,128]{1,0:T(8,128)(2,1)}, bf16[2304,128]{1,0:T(8,128)(2,1)}, bf16[2304,128]{1,0:T(8,128)(2,1)}, ...) custom-call(s32[35]{0:T(128)} %pad_add_fusion.1.meta, ...), custom_call_target="tpu_custom_call" | custom-call | flops 11811160064 | bytes 15073280 | tf_op jit(solution)/shard_map/attention/pallas_call | solution.py:285
  139.1 32.5 %attention.3 = (bf16[2,2048,576]{2,1,0:T(8,128)(2,1)}, bf16[1024,128]{1,0:T(8,128)(2,1)}, bf16[2304,128]{1,0:T(8,128)(2,1)}, bf16[2304,128]{1,0:T(8,128)(2,1)}, ...) custom-call(s32[35]{0:T(128)} %pad_add_fusion.1.meta, ...), custom_call_target="tpu_custom_call", output_to_operand_aliasing={{0}: (12, {})} | custom-call | flops 11811160064 | bytes 15073280 | tf_op jit(solution)/shard_map/attention/pallas_call | solution.py:285
  171.6 8.5 %collective-permute-start.15 = (f32[32,1024]{1,0:T(8,128)}, f32[32,1024]{1,0:T(8,128)S(1)}, u32[]{:S(2)}, u32[]{:S(2)}) collective-permute-start(f32[32,1024]{1,0:T(8,128)} %get-tuple-element.55), channel_id=1, source_target_pairs={{0,4},{4,8},{8,12},{12,0},{1,5},{5,9},{9,13},{13,1},{2,6},{6,10},{... | collective-permute-start | bytes 393224 | tf_op jit(solution)/shard_map/ppermute | solution.py:531
  180.1 5.7 %collective-permute-start.16 = (f32[32,1024]{1,0:T(8,128)}, f32[32,1024]{1,0:T(8,128)S(1)}, u32[]{:S(2)}, u32[]{:S(2)}) collective-permute-start(f32[32,1024]{1,0:T(8,128)} %get-tuple-element.56), channel_id=1, source_target_pairs={{0,8},{4,12},{8,0},{12,4},{1,9},{5,13},{9,1},{13,5},{2,10},{6,14},... | collective-permute-start | bytes 393224 | tf_op jit(solution)/shard_map/ppermute | solution.py:531
  185.9 5.7 %collective-permute-start.17 = (f32[32,1024]{1,0:T(8,128)}, f32[32,1024]{1,0:T(8,128)S(1)}, u32[]{:S(2)}, u32[]{:S(2)}) collective-permute-start(f32[32,1024]{1,0:T(8,128)} %get-tuple-element.57), channel_id=1, source_target_pairs={{0,12},{4,0},{8,4},{12,8},{1,13},{5,1},{9,5},{13,9},{2,14},{6,2},{... | collective-permute-start | bytes 393224 | tf_op jit(solution)/shard_map/ppermute | solution.py:531
  218.0 8.2 %collective-permute-done.19.refs_6_ = f32[2,16,1024]{2,1,0:T(8,128)S(1)} collective-permute-done((f32[2,16,1024]{2,1,0:T(8,128)}, f32[2,16,1024]{2,1,0:T(8,128)S(1)}, u32[]{:S(2)}, u32[]{:S(2)}) %collective-permute-start.19) | collective-permute-done | bytes 131104 | tf_op jit(solution)/shard_map/ppermute | solution.py:531
  226.9 10.2 %indexer.1 = (bf16[2,1024,128]{2,1,0:T(8,128)(2,1)}, f32[2,1024,1]{2,1,0:T(8,128)}, bf16[2,512,128]{2,1,0:T(8,128)(2,1)}, bf16[2,512,128]{2,1,0:T(8,128)(2,1)}, ...) custom-call(s32[35]{0:T(128)} %pad_add_fusion.1.meta, ...), custom_call_target="tpu_custom_call" | custom-call | flops 1610612736 | bytes 4194304 | tf_op jit(solution)/shard_map/indexer/pallas_call | solution.py:409
  253.1 5.4 %collective-permute-done.27 = bf16[2304,128]{1,0:T(8,128)(2,1)S(1)} collective-permute-done((bf16[2304,128]{1,0:T(8,128)(2,1)S(1)}, bf16[2304,128]{1,0:T(8,128)(2,1)S(1)}, u32[]{:S(2)}, u32[]{:S(2)}) %collective-permute-start.27) | collective-permute-done | bytes 589856 | tf_op jit(solution)/shard_map/ppermute | solution.py:522
  264.8 6.4 %collective-permute-done.21 = bf16[2304,128]{1,0:T(8,128)(2,1)S(1)} collective-permute-done((bf16[2304,128]{1,0:T(8,128)(2,1)S(1)}, bf16[2304,128]{1,0:T(8,128)(2,1)S(1)}, u32[]{:S(2)}, u32[]{:S(2)}) %collective-permute-start.21) | collective-permute-done | bytes 589856 | tf_op jit(solution)/shard_map/ppermute | solution.py:522
  283.6 5.8 %collective-permute-done.28 = bf16[2304,128]{1,0:T(8,128)(2,1)S(1)} collective-permute-done((bf16[2304,128]{1,0:T(8,128)(2,1)S(1)}, bf16[2304,128]{1,0:T(8,128)(2,1)S(1)}, u32[]{:S(2)}, u32[]{:S(2)}) %collective-permute-start.28) | collective-permute-done | bytes 589856 | tf_op jit(solution)/shard_map/ppermute | solution.py:522
  296.3 5.8 %collective-permute-done.22 = bf16[2304,128]{1,0:T(8,128)(2,1)S(1)} collective-permute-done((bf16[2304,128]{1,0:T(8,128)(2,1)S(1)}, bf16[2304,128]{1,0:T(8,128)(2,1)S(1)}, u32[]{:S(2)}, u32[]{:S(2)}) %collective-permute-start.22) | collective-permute-done | bytes 589856 | tf_op jit(solution)/shard_map/ppermute | solution.py:522
  308.9 11.4 %collective-permute-done.29 = bf16[2304,128]{1,0:T(8,128)(2,1)S(1)} collective-permute-done((bf16[2304,128]{1,0:T(8,128)(2,1)S(1)}, bf16[2304,128]{1,0:T(8,128)(2,1)S(1)}, u32[]{:S(2)}, u32[]{:S(2)}) %collective-permute-start.29) | collective-permute-done | bytes 589856 | tf_op jit(solution)/shard_map/ppermute | solution.py:522
  321.9 6.7 %collective-permute-start.34 = (bf16[2304,128]{1,0:T(8,128)(2,1)S(1)}, bf16[2304,128]{1,0:T(8,128)(2,1)S(1)}, u32[]{:S(2)}, u32[]{:S(2)}) collective-permute-start(bf16[2304,128]{1,0:T(8,128)(2,1)S(1)} %add_convert_fusion.refs_1_), channel_id=1, source_target_pairs={{0,2},{1,3},{2,0},{3,1},{4,6},{5,7},{6,4},{7,5},{8,10},{9,11},{10,... | collective-permute-start | bytes 1769480 | tf_op jit(solution)/shard_map/ppermute | solution.py:531
  337.7 7.0 %collective-permute-done.34.refs_3_ = bf16[2304,128]{1,0:T(8,128)(2,1)S(1)} collective-permute-done((bf16[2304,128]{1,0:T(8,128)(2,1)S(1)}, bf16[2304,128]{1,0:T(8,128)(2,1)S(1)}, u32[]{:S(2)}, u32[]{:S(2)}) %collective-permute-start.34) | collective-permute-done | bytes 589856 | tf_op jit(solution)/shard_map/ppermute | solution.py:531
  344.7 12.3 %collective-permute-done.33.refs_2_ = bf16[2304,128]{1,0:T(8,128)(2,1)} collective-permute-done((bf16[2304,128]{1,0:T(8,128)(2,1)S(1)}, bf16[2304,128]{1,0:T(8,128)(2,1)}, u32[]{:S(2)}, u32[]{:S(2)}) %collective-permute-start.33) | collective-permute-done | bytes 589856 | tf_op jit(solution)/shard_map/ppermute | solution.py:531
  358.8 7.0 %all-reduce = s32[136]{0:T(256)S(1)} all-reduce(s32[136]{0:T(256)S(1)} %add_dynamic-update-slice_fusion), channel_id=2, replica_groups=mesh['rep'=2,'ctx'=4,'smp'=4] {'smp'}, use_global_device_ids=true, to_apply=%add | all-reduce | flops 136 | bytes 1088
  367.7 5.7 %settle.1 = (bf16[2048,576]{1,0:T(8,128)(2,1)}, bf16[2048,128]{1,0:T(8,128)(2,1)}) custom-call(s32[138]{0:T(256)} %pad_add_fusion.here, bf16[2304,128]{1,0:T(8,128)(2,1)} %copy-done.1, bf16[2304,128]{1,0:T(8,128)(2,1)} %copy-done, bf16[2304,128]{1,0:T(8,128)(2,1)} %collective-permute-done.33.refs_2_, bf16[2304,128]{1,0:T(8,128)(2,1)} %copy-done.4, ...), custom_call_target="tpu_custom_call" | custom-call | bytes 9437184 | tf_op jit(solution)/shard_map/settle/pallas_call | solution.py:488
  (195 shorter events, 120.0 us)
Async XLA Ops:
  27.4 30.6 %collective-permute-start.3 = (bf16[2816,128]{1,0:T(8,128)(2,1)}, bf16[2816,128]{1,0:T(8,128)(2,1)S(1)}, u32[]{:S(2)}, u32[]{:S(2)}) collective-permute-start(bf16[2816,128]{1,0:T(8,128)(2,1)} %get-tuple-element.44.refs_4_), channel_id=1, source_target_pairs={{4,0},{8,4},{12,8},{5,1},{9,5},{13,9},{6,2},{10,6},{14,10},{7,3},{... | collective-permute-start | bytes 2162696 | tf_op jit(solution)/shard_map/ppermute | solution.py:508
  28.7 30.6 %collective-permute-start = (bf16[2816,128]{1,0:T(8,128)(2,1)}, bf16[2816,128]{1,0:T(8,128)(2,1)S(1)}, u32[]{:S(2)}, u32[]{:S(2)}) collective-permute-start(bf16[2816,128]{1,0:T(8,128)(2,1)} %get-tuple-element.44.refs_4_), channel_id=1, source_target_pairs={{0,4},{4,8},{8,12},{1,5},{5,9},{9,13},{2,6},{6,10},{10,14},{3,7},{... | collective-permute-start | bytes 2162696 | tf_op jit(solution)/shard_map/ppermute | solution.py:507
  42.6 31.0 %collective-permute-start.10 = (bf16[2816,128]{1,0:T(8,128)(2,1)S(1)}, bf16[2816,128]{1,0:T(8,128)(2,1)}, u32[]{:S(2)}, u32[]{:S(2)}) collective-permute-start(bf16[2816,128]{1,0:T(8,128)(2,1)S(1)} %collective-permute-done.9.refs_8_), channel_id=1, source_target_pairs={{4,0},{8,4},{5,1},{9,5},{6,2},{10,6},{7,3},{11,7},{20,16},{24,20},... | collective-permute-start | bytes 2162696 | tf_op jit(solution)/shard_map/ppermute | solution.py:508
  44.2 30.7 %collective-permute-start.7 = (bf16[2816,128]{1,0:T(8,128)(2,1)S(1)}, bf16[2816,128]{1,0:T(8,128)(2,1)}, u32[]{:S(2)}, u32[]{:S(2)}) collective-permute-start(bf16[2816,128]{1,0:T(8,128)(2,1)S(1)} %collective-permute-done.6.refs_5_), channel_id=1, source_target_pairs={{4,8},{8,12},{5,9},{9,13},{6,10},{10,14},{7,11},{11,15},{20,24},{2... | collective-permute-start | bytes 2162696 | tf_op jit(solution)/shard_map/ppermute | solution.py:507
  58.0 31.0 %collective-permute-start.4 = (bf16[2816,128]{1,0:T(8,128)(2,1)S(1)}, bf16[2816,128]{1,0:T(8,128)(2,1)}, u32[]{:S(2)}, u32[]{:S(2)}) collective-permute-start(bf16[2816,128]{1,0:T(8,128)(2,1)S(1)} %collective-permute-done.3.refs_8_), channel_id=1, source_target_pairs={{4,0},{8,4},{5,1},{9,5},{6,2},{10,6},{7,3},{11,7},{20,16},{24,20},... | collective-permute-start | bytes 2162696 | tf_op jit(solution)/shard_map/ppermute | solution.py:508
  59.3 31.0 %collective-permute-start.1 = (bf16[2816,128]{1,0:T(8,128)(2,1)S(1)}, bf16[2816,128]{1,0:T(8,128)(2,1)}, u32[]{:S(2)}, u32[]{:S(2)}) collective-permute-start(bf16[2816,128]{1,0:T(8,128)(2,1)S(1)} %collective-permute-done.refs_5_), channel_id=1, source_target_pairs={{4,8},{8,12},{5,9},{9,13},{6,10},{10,14},{7,11},{11,15},{20,24},{2... | collective-permute-start | bytes 2162696 | tf_op jit(solution)/shard_map/ppermute | solution.py:507
  73.6 30.9 %collective-permute-start.11 = (bf16[2816,128]{1,0:T(8,128)(2,1)}, bf16[2816,128]{1,0:T(8,128)(2,1)}, u32[]{:S(2)}, u32[]{:S(2)}) collective-permute-start(bf16[2816,128]{1,0:T(8,128)(2,1)} %collective-permute-done.10.refs_9_), channel_id=1, source_target_pairs={{4,0},{5,1},{6,2},{7,3},{20,16},{21,17},{22,18},{23,19}} | collective-permute-start | bytes 2162696 | tf_op jit(solution)/shard_map/ppermute | solution.py:508
  74.9 29.6 %collective-permute-start.8 = (bf16[2816,128]{1,0:T(8,128)(2,1)}, bf16[2816,128]{1,0:T(8,128)(2,1)}, u32[]{:S(2)}, u32[]{:S(2)}) collective-permute-start(bf16[2816,128]{1,0:T(8,128)(2,1)} %collective-permute-done.7.refs_6_), channel_id=1, source_target_pairs={{8,12},{9,13},{10,14},{11,15},{24,28},{25,29},{26,30},{27,31}} | collective-permute-start | bytes 2162696 | tf_op jit(solution)/shard_map/ppermute | solution.py:507
  89.0 48.9 %collective-permute-start.5 = (bf16[2816,128]{1,0:T(8,128)(2,1)}, bf16[2816,128]{1,0:T(8,128)(2,1)S(1)}, u32[]{:S(2)}, u32[]{:S(2)}) collective-permute-start(bf16[2816,128]{1,0:T(8,128)(2,1)} %collective-permute-done.4.refs_9_), channel_id=1, source_target_pairs={{4,0},{5,1},{6,2},{7,3},{20,16},{21,17},{22,18},{23,19}} | collective-permute-start | bytes 2162696 | tf_op jit(solution)/shard_map/ppermute | solution.py:508
  90.3 47.7 %collective-permute-start.2 = (bf16[2816,128]{1,0:T(8,128)(2,1)}, bf16[2816,128]{1,0:T(8,128)(2,1)S(1)}, u32[]{:S(2)}, u32[]{:S(2)}) collective-permute-start(bf16[2816,128]{1,0:T(8,128)(2,1)} %collective-permute-done.1.refs_6_), channel_id=1, source_target_pairs={{8,12},{9,13},{10,14},{11,15},{24,28},{25,29},{26,30},{27,31}} | collective-permute-start | bytes 2162696 | tf_op jit(solution)/shard_map/ppermute | solution.py:507
  171.6 24.3 %collective-permute-start.15 = (f32[32,1024]{1,0:T(8,128)}, f32[32,1024]{1,0:T(8,128)S(1)}, u32[]{:S(2)}, u32[]{:S(2)}) collective-permute-start(f32[32,1024]{1,0:T(8,128)} %get-tuple-element.55), channel_id=1, source_target_pairs={{0,4},{4,8},{8,12},{12,0},{1,5},{5,9},{9,13},{13,1},{2,6},{6,10},{... | collective-permute-start | bytes 393224 | tf_op jit(solution)/shard_map/ppermute | solution.py:531
  241.9 29.2 %collective-permute-start.21 = (bf16[2304,128]{1,0:T(8,128)(2,1)S(1)}, bf16[2304,128]{1,0:T(8,128)(2,1)S(1)}, u32[]{:S(2)}, u32[]{:S(2)}) collective-permute-start(bf16[2304,128]{1,0:T(8,128)(2,1)S(1)} %copy-done.34), channel_id=1, source_target_pairs={{0,4},{1,5},{2,6},{3,7},{16,20},{17,21},{18,22},{19,23}} | collective-permute-start | bytes 1769480 | tf_op jit(solution)/shard_map/ppermute | solution.py:522
  246.0 26.1 %collective-permute-start.24 = (bf16[2304,128]{1,0:T(8,128)(2,1)S(1)}, bf16[2304,128]{1,0:T(8,128)(2,1)S(1)}, u32[]{:S(2)}, u32[]{:S(2)}) collective-permute-start(bf16[2304,128]{1,0:T(8,128)(2,1)S(1)} %copy-done.33), channel_id=1, source_target_pairs={{12,8},{13,9},{14,10},{15,11},{28,24},{29,25},{30,26},{31,27}} | collective-permute-start | bytes 1769480 | tf_op jit(solution)/shard_map/ppermute | solution.py:523
  247.7 29.7 %collective-permute-start.40 = (bf16[2,512,128]{2,1,0:T(8,128)(2,1)S(1)}, bf16[2,512,128]{2,1,0:T(8,128)(2,1)S(1)}, u32[]{:S(2)}, u32[]{:S(2)}) collective-permute-start(bf16[2,512,128]{2,1,0:T(8,128)(2,1)S(1)} %add_convert_fusion.14), channel_id=1, source_target_pairs={{0,4},{4,8},{1,5},{5,9},{2,6},{6,10},{3,7},{7,11},{16,20},{20,24},... | collective-permute-start | bytes 786440 | tf_op jit(solution)/shard_map/ppermute | solution.py:522
  259.4 30.0 %collective-permute-start.28 = (bf16[2304,128]{1,0:T(8,128)(2,1)S(1)}, bf16[2304,128]{1,0:T(8,128)(2,1)S(1)}, u32[]{:S(2)}, u32[]{:S(2)}) collective-permute-start(bf16[2304,128]{1,0:T(8,128)(2,1)S(1)} %add_convert_fusion.4), channel_id=1, source_target_pairs={{0,4},{4,8},{1,5},{5,9},{2,6},{6,10},{3,7},{7,11},{16,20},{20,24},... | collective-permute-start | bytes 1769480 | tf_op jit(solution)/shard_map/ppermute | solution.py:522
  272.1 30.0 %collective-permute-start.22 = (bf16[2304,128]{1,0:T(8,128)(2,1)S(1)}, bf16[2304,128]{1,0:T(8,128)(2,1)S(1)}, u32[]{:S(2)}, u32[]{:S(2)}) collective-permute-start(bf16[2304,128]{1,0:T(8,128)(2,1)S(1)} %add_convert_fusion.9), channel_id=1, source_target_pairs={{0,4},{4,8},{1,5},{5,9},{2,6},{6,10},{3,7},{7,11},{16,20},{20,24},... | collective-permute-start | bytes 1769480 | tf_op jit(solution)/shard_map/ppermute | solution.py:522
  277.4 26.1 %collective-permute-start.25 = (bf16[2304,128]{1,0:T(8,128)(2,1)S(1)}, bf16[2304,128]{1,0:T(8,128)(2,1)S(1)}, u32[]{:S(2)}, u32[]{:S(2)}) collective-permute-start(bf16[2304,128]{1,0:T(8,128)(2,1)S(1)} %add_convert_fusion.7), channel_id=1, source_target_pairs={{8,4},{12,8},{9,5},{13,9},{10,6},{14,10},{11,7},{15,11},{24,20},{2... | collective-permute-start | bytes 1769480 | tf_op jit(solution)/shard_map/ppermute | solution.py:523
  278.4 58.5 %collective-permute-start.41 = (bf16[2,512,128]{2,1,0:T(8,128)(2,1)S(1)}, bf16[2,512,128]{2,1,0:T(8,128)(2,1)S(1)}, u32[]{:S(2)}, u32[]{:S(2)}) collective-permute-start(bf16[2,512,128]{2,1,0:T(8,128)(2,1)S(1)} %add_convert_fusion.13), channel_id=1, source_target_pairs={{0,4},{4,8},{8,12},{1,5},{5,9},{9,13},{2,6},{6,10},{10,14},{3,7},{... | collective-permute-start | bytes 786440 | tf_op jit(solution)/shard_map/ppermute | solution.py:522
  289.4 47.5 %collective-permute-start.44 = (bf16[2,512,128]{2,1,0:T(8,128)(2,1)S(1)}, bf16[2,512,128]{2,1,0:T(8,128)(2,1)S(1)}, u32[]{:S(2)}, u32[]{:S(2)}) collective-permute-start(bf16[2,512,128]{2,1,0:T(8,128)(2,1)S(1)} %add_convert_fusion.11), channel_id=1, source_target_pairs={{4,0},{8,4},{12,8},{5,1},{9,5},{13,9},{6,2},{10,6},{14,10},{7,3},{... | collective-permute-start | bytes 786440 | tf_op jit(solution)/shard_map/ppermute | solution.py:523
  290.9 29.4 %collective-permute-start.29 = (bf16[2304,128]{1,0:T(8,128)(2,1)S(1)}, bf16[2304,128]{1,0:T(8,128)(2,1)S(1)}, u32[]{:S(2)}, u32[]{:S(2)}) collective-permute-start(bf16[2304,128]{1,0:T(8,128)(2,1)S(1)} %add_convert_fusion.3), channel_id=1, source_target_pairs={{0,4},{4,8},{8,12},{1,5},{5,9},{9,13},{2,6},{6,10},{10,14},{3,7},{... | collective-permute-start | bytes 1769480 | tf_op jit(solution)/shard_map/ppermute | solution.py:522
  303.5 27.7 %collective-permute-start.23 = (bf16[2304,128]{1,0:T(8,128)(2,1)S(1)}, bf16[2304,128]{1,0:T(8,128)(2,1)S(1)}, u32[]{:S(2)}, u32[]{:S(2)}) collective-permute-start(bf16[2304,128]{1,0:T(8,128)(2,1)S(1)} %add_convert_fusion.8), channel_id=1, source_target_pairs={{0,4},{4,8},{8,12},{1,5},{5,9},{9,13},{2,6},{6,10},{10,14},{3,7},{... | collective-permute-start | bytes 1769480 | tf_op jit(solution)/shard_map/ppermute | solution.py:522
  337.1 30.6 %collective-permute-start.36 = (bf16[2304,128]{1,0:T(8,128)(2,1)S(1)}, bf16[2304,128]{1,0:T(8,128)(2,1)}, u32[]{:S(2)}, u32[]{:S(2)}) collective-permute-start(bf16[2304,128]{1,0:T(8,128)(2,1)S(1)} %add_convert_fusion.refs_1_), channel_id=1, source_target_pairs={{0,1},{1,0},{2,3},{3,2},{4,5},{5,4},{6,7},{7,6},{8,9},{9,8},{10,11... | collective-permute-start | bytes 1769480 | tf_op jit(solution)/shard_map/ppermute | solution.py:536
  337.6 30.1 %collective-permute-start.35 = (bf16[2304,128]{1,0:T(8,128)(2,1)S(1)}, bf16[2304,128]{1,0:T(8,128)(2,1)}, u32[]{:S(2)}, u32[]{:S(2)}) collective-permute-start(bf16[2304,128]{1,0:T(8,128)(2,1)S(1)} %add_convert_fusion.5.refs_0_), channel_id=1, source_target_pairs={{0,1},{1,0},{2,3},{3,2},{4,5},{5,4},{6,7},{7,6},{8,9},{9,8},{10,11... | collective-permute-start | bytes 1769480 | tf_op jit(solution)/shard_map/ppermute | solution.py:536
  344.6 23.0 %collective-permute-start.38 = (bf16[2304,128]{1,0:T(8,128)(2,1)S(1)}, bf16[2304,128]{1,0:T(8,128)(2,1)}, u32[]{:S(2)}, u32[]{:S(2)}) collective-permute-start(bf16[2304,128]{1,0:T(8,128)(2,1)S(1)} %collective-permute-done.34.refs_3_), channel_id=1, source_target_pairs={{0,1},{1,0},{2,3},{3,2},{4,5},{5,4},{6,7},{7,6},{8,9},{9,8},{10,11... | collective-permute-start | bytes 1769480 | tf_op jit(solution)/shard_map/ppermute | solution.py:536
  (68 other events, 1305.4 us)

commit v2 on v1

v2 whole, which is shorter than its diff:
```python
import functools

import jax
import jax.numpy as jnp
from jax import lax
from jax.experimental import pallas as pl
from jax.experimental.pallas import tpu as pltpu
from jax.sharding import PartitionSpec as P

H = 128
BLK = 64
HALF = BLK // 2
LANE = 128

SCALE = 192.0 ** (-0.5)
IDX_SCALE = 128.0 ** (-0.5)
LOSS = 256.0
NEG = -1e30
EXACT = lax.Precision.HIGHEST
VMEM_BYTES = 56 * 1024 * 1024

NT = (((1,), (1,)), ((), ()))
F32 = jnp.float32
BF16 = jnp.bfloat16


def params():
    return pltpu.CompilerParams(vmem_limit_bytes=VMEM_BYTES)


def cost(flops, moved):
    return pl.CostEstimate(flops=int(flops), bytes_accessed=int(moved), transcendentals=0)


def any_spec():
    return pl.BlockSpec(memory_space=pl.ANY)


def vmem_spec():
    return pl.BlockSpec(memory_space=pltpu.VMEM)


def smem_spec():
    return pl.BlockSpec(memory_space=pltpu.SMEM)


def below(meta, base, listed, number, bound):
    total = jnp.int32(0)
    for i in range(listed):
        total += jnp.where((i < number) & (meta[base + i] < bound), 1, 0)
    return total


def span(meta, base, listed, number, shard, per_shard):
    first = below(meta, base, listed, number, shard * per_shard)
    last = below(meta, base, listed, number, (shard + 1) * per_shard)
    return first, last - first


def pack_kernel(dims, meta, kv_t, ik, *rest):
    samples, listed, slots, per_shard, width, tiles = dims
    outs, (kbuf, ibuf, sem) = rest[:samples], rest[samples:]
    me = meta[samples * (listed + 1)]
    copies, sides = [], []
    for s in range(samples):
        number = meta[samples * listed + s]
        first, _ = span(meta, s * listed, listed, number, me, per_shard)
        for j in range(slots):
            at = s * slots + j
            place = jnp.minimum(first + j, listed - 1)
            block = jnp.clip(meta[s * listed + place] - me * per_shard, 0, per_shard - 1)
            rows = pl.ds(pl.multiple_of(block * BLK, BLK), BLK)
            pair = pl.ds(pl.multiple_of(block // 2 * LANE, LANE), LANE)
            one = pltpu.make_async_copy(kv_t.at[:, pair], kbuf.at[at], sem.at[at, 0])
            two = pltpu.make_async_copy(ik.at[rows], ibuf.at[at], sem.at[at, 1])
            one.start()
            two.start()
            copies.append((one, two))
            sides.append(lax.rem(block, 2) == 0)
    for at in range(samples * slots):
        out, j = outs[at // slots], at % slots
        copies[at][0].wait()
        copies[at][1].wait()
        for c in range(tiles):
            both = kbuf[at, c * LANE : (c + 1) * LANE, :].T
            out[pl.ds((c * slots + j) * BLK, BLK), :] = jnp.where(sides[at], both[:BLK], both[BLK:])
        out[pl.ds((tiles * slots + j) * BLK, BLK), :] = ibuf[at]
        both = kbuf[at, tiles * LANE : width, :].T
        tail = jnp.where(sides[at], both[:BLK], both[BLK:])
        out[pl.ds((tiles + 1) * slots * BLK + j * HALF, HALF), :] = jnp.concatenate(
            [tail[:HALF], tail[HALF:]], axis=1
        )


def pack(meta, kv_t, ik, dims):
    samples, listed, slots, per_shard, width, tiles = dims
    rows = slots * ((tiles + 1) * BLK + HALF)
    return pl.pallas_call(
        functools.partial(pack_kernel, dims),
        out_shape=[jax.ShapeDtypeStruct((rows, LANE), BF16)] * samples,
        in_specs=[smem_spec(), any_spec(), any_spec()],
        out_specs=[vmem_spec()] * samples,
        scratch_shapes=[
            pltpu.VMEM((samples * slots, width, LANE), BF16),
            pltpu.VMEM((samples * slots, BLK, ik.shape[1]), BF16),
            pltpu.SemaphoreType.DMA((samples * slots, 2)),
        ],
        compiler_params=params(),
        cost_estimate=cost(0, 4 * samples * rows * LANE * 2),
        name="pack",
    )(meta, kv_t, ik)


def shard_of(at, me, n_ctx):
    if at == 0:
        return me
    return me - at if at < n_ctx else me + (at - n_ctx + 1)


def unpack_slab(slab, first, many, slots, tiles, k_ref, ikey_ref):
    value, side = tiles * LANE, LANE // 2

    def place(j, _):
        to = pl.multiple_of((first + j) * BLK, BLK)
        for c in range(tiles + 1):
            piece = slab[pl.ds(pl.multiple_of((c * slots + j) * BLK, BLK), BLK), :]
            if c < tiles:
                k_ref[pl.ds(to, BLK), c * LANE : (c + 1) * LANE] = piece
            else:
                ikey_ref[pl.ds(to, BLK), :] = piece
        piece = slab[pl.ds(pl.multiple_of((tiles + 1) * slots * BLK + j * HALF, HALF), HALF), :]
        k_ref[pl.ds(to, HALF), value : value + side] = piece[:, :side]
        k_ref[pl.ds(pl.multiple_of(to + HALF, HALF), HALF), value : value + side] = piece[:, side:]
        return 0

    lax.fori_loop(0, many, place, 0)


def emit_slab(acc, out, first, many, slots, tiles):
    value, side = tiles * LANE, LANE // 2

    def emit(j, _):
        rows = pl.ds(pl.multiple_of((first + j) * BLK, BLK), BLK)
        for c in range(tiles):
            out[pl.ds(pl.multiple_of((c * slots + j) * BLK, BLK), BLK), :] = acc[
                rows, c * LANE : (c + 1) * LANE
            ].astype(BF16)
        tail = acc[rows, value : value + side].astype(BF16)
        out[pl.ds(pl.multiple_of(tiles * slots * BLK + j * HALF, HALF), HALF), :] = (
            jnp.concatenate([tail[:HALF], tail[HALF:]], axis=1)
        )
        return 0

    lax.fori_loop(0, many, emit, 0)


def attention_kernel(dims, s, n_ctx, heads, groups, lo, opens, closes, riding, extra, meta, *refs):
    samples, listed, slots, per_shard, width, tiles = dims
    near = 2 * n_ctx - 1
    refs = list(refs)

    def take(count):
        head = refs[:count]
        del refs[:count]
        return head

    q_ref, do_ref, iq_ref, wcol_ref = take(4)
    slabs = take(near) if opens else []
    carried = [] if opens else take(6)
    riders = take(riding)
    take(extra)
    (dq_ref,) = take(1)
    if closes:
        outs, parts = take(near), take(n_ctx)
    if opens:
        ikey_ref, k_ref, kt_ref, acc, mass_t, logits = take(6)
    else:
        ikey_ref, k_ref, kt_ref = carried[:3]
        acc, mass_t, logits = take(3)
    step = pl.program_id(0)
    value = tiles * LANE
    keys = listed * BLK
    rows = q_ref.shape[0]
    times = rows // heads
    every = mass_t.shape[1]
    me = meta[samples * (listed + 1)]
    number = meta[samples * listed + s]
    live = number * BLK

    @pl.when(step == 0)
    def _():
        if not opens:
            acc[...] = carried[3][...]
            mass_t[...] = carried[4][...]
            logits[...] = carried[5][...]
            return
        for at in range(near):
            first, many = span(
                meta, s * listed, listed, number, shard_of(at, me, n_ctx), per_shard
            )
            unpack_slab(slabs[at], first, many, slots, tiles, k_ref, ikey_ref)

        def clear(i, _):
            to = pl.multiple_of(i * BLK, BLK)
            k_ref[pl.ds(to, BLK), :] = jnp.zeros((BLK, k_ref.shape[1]), BF16)
            ikey_ref[pl.ds(to, BLK), :] = jnp.zeros((BLK, ikey_ref.shape[1]), BF16)
            return 0

        lax.fori_loop(number, listed, clear, 0)
        k_ref[:, width:] = jnp.zeros((keys, k_ref.shape[1] - width), BF16)
        kt_ref[...] = k_ref[...].T
        acc[...] = jnp.zeros_like(acc)
        mass_t[...] = jnp.zeros_like(mass_t)
        logits[...] = jnp.zeros_like(logits)

    q = q_ref[...]
    do = do_ref[...]
    scores = lax.dot_general(k_ref[:, :width], q, NT, preferred_element_type=F32)
    alive = lax.broadcasted_iota(jnp.int32, (keys, 1), 0) < live
    scores = jnp.where(alive, scores * SCALE, NEG)
    expo = jnp.exp(scores - jnp.max(scores, axis=0, keepdims=True))
    probs = expo * (1.0 / jnp.sum(expo, axis=0, keepdims=True))
    probs_b = probs.astype(BF16)
    dprob = lax.dot_general(k_ref[:, :value], do, NT, preferred_element_type=F32)
    delta = jnp.sum(probs * dprob, axis=0, keepdims=True)
    dscore = (probs * (dprob - delta) * SCALE).astype(BF16)
    dq_t = jnp.dot(kt_ref[...], dscore, preferred_element_type=F32)
    dq_ref[...] = dq_t.T[:, :width].astype(BF16)
    acc[:, :width] += jnp.dot(dscore, q, preferred_element_type=F32)
    acc[:, :value] += jnp.dot(probs_b, do, preferred_element_type=F32)
    row = lax.broadcasted_iota(jnp.int32, (rows, every), 0) // heads + (lo + step) * times
    column = lax.broadcasted_iota(jnp.int32, (rows, every), 1)
    member = jnp.where(row == column, 1.0, 0.0).astype(BF16)
    mass_t[...] += jnp.dot(probs_b, member, preferred_element_type=F32)

    inner = lax.dot_general(iq_ref[...], ikey_ref[...], NT, preferred_element_type=F32)
    weighed = jnp.maximum(inner, 0.0) * (wcol_ref[...] * IDX_SCALE)
    if groups % 8 == 0:
        logit = jnp.sum(weighed.reshape(times, groups, keys), axis=1)
    else:
        fold = (
            lax.broadcasted_iota(jnp.int32, (times, times * groups), 1) // groups
            == lax.broadcasted_iota(jnp.int32, (times, times * groups), 0)
        ).astype(F32)
        logit = jnp.dot(fold, weighed, precision=EXACT, preferred_element_type=F32)
    logits[pl.ds(pl.multiple_of((lo + step) * times, times), times), :] = logit

    if closes:

        @pl.when(step == pl.num_programs(0) - 1)
        def _():
            for at in range(near):
                first, many = span(
                    meta, s * listed, listed, number, shard_of(at, me, n_ctx), per_shard
                )
                emit_slab(acc, outs[at], first, many, slots, tiles)
            mass = mass_t[...].T
            part = every // n_ctx
            behind = riders[0].shape[0] if riding else 0
            for k in range(riding):
                parts[k][:behind] = riders[k][...]
            for c in range(n_ctx):
                to = lax.rem(c - me + n_ctx, n_ctx)
                here = slice(c * part, (c + 1) * part)
                for k in range(n_ctx):

                    @pl.when(to == k)
                    def _(here=here, k=k):
                        parts[k][behind : behind + part] = mass[here]
                        parts[k][behind + part :] = logits[here, :]


def attention(meta, query, dout, idx_query, wcol, slabs, state, riders, d_query, dims, s, n_ctx,
              heads, tall, lo, hi, after):
    samples, listed, slots, per_shard, width, tiles = dims
    total = query.shape[1]
    every = total // heads
    groups = idx_query.shape[1] // every
    ind = idx_query.shape[2]
    side = tall // heads * groups
    value = tiles * LANE
    keys = listed * BLK
    wide = (width + LANE - 1) // LANE * LANE
    near = 2 * n_ctx - 1
    opens, closes = lo == 0, hi == total // tall
    grad_rows = slots * (tiles * BLK + HALF)

    def row_spec(size, columns):
        return pl.BlockSpec((None, size, columns), lambda i: (s, lo + i, 0))

    def whole(shape):
        return pl.BlockSpec(shape, lambda i: (0,) * len(shape))

    args = [meta, query, dout, idx_query, wcol]
    in_specs = [
        smem_spec(), row_spec(tall, width), row_spec(tall, value), row_spec(side, ind),
        row_spec(side, 1),
    ]
    if opens:
        args += slabs
        in_specs += [whole(slabs[0].shape)] * near
    else:
        args += state
        in_specs += [whole(x.shape) for x in state]
    args += riders
    in_specs += [whole(x.shape) for x in riders]
    aliases = {}
    if d_query is not None:
        aliases = {len(args): 0}
        args.append(d_query)
        in_specs.append(any_spec())
    args += after
    in_specs += [any_spec()] * len(after)
    store = [
        ((keys, ind), BF16), ((keys, wide), BF16), ((wide, keys), BF16), ((keys, wide), F32),
        ((keys, every), F32), ((every, keys), F32),
    ]
    out_shape = [(query.shape, BF16)]
    out_specs = [row_spec(tall, width)]
    scratch = []
    if closes:
        out_shape += [((grad_rows, LANE), BF16)] * near
        behind = riders[0].shape[0] if riders else 0
        out_shape += [((behind + 2 * (every // n_ctx), keys), F32)] * n_ctx
    kept = len(out_shape)
    if opens:
        out_shape += store[:1] if closes else store
    if closes:
        scratch = [pltpu.VMEM(*x) for x in (store[1:] if opens else store[3:])]
    out_specs += [whole(x[0]) for x in out_shape[1:]]
    count = (hi - lo) * tall
    out = pl.pallas_call(
        functools.partial(
            attention_kernel, dims, s, n_ctx, heads, groups, lo, opens, closes,
            len(riders), len(aliases) + len(after),
        ),
        grid=(hi - lo,),
        out_shape=[jax.ShapeDtypeStruct(*x) for x in out_shape],
        in_specs=in_specs,
        out_specs=out_specs,
        scratch_shapes=scratch,
        input_output_aliases=aliases,
        compiler_params=params(),
        cost_estimate=cost(
            2 * count * keys * (3 * width + 2 * value),
            count * (2 * width + value) * 2 + 14 * grad_rows * LANE * 2,
        ),
        name="attention",
    )(*args)
    if not closes:
        return out[0], list(out[1:])
    ikey = out[kept] if opens else state[0]
    return out[0], list(out[1 : 1 + near]), list(out[1 + near : kept]), ikey


def divergence_kernel(samples, listed, n_ctx, meta, *refs):
    out = refs[-1]
    part, keys = out.shape[1:]
    total = refs[0][...]
    for k in range(1, n_ctx):
        total += refs[k][...]
    for s in range(samples):
        mass = total[2 * s * part : (2 * s + 1) * part]
        alive = lax.broadcasted_iota(jnp.int32, (1, keys), 1) < meta[samples * listed + s] * BLK
        logit = jnp.where(alive, total[(2 * s + 1) * part : (2 * s + 2) * part], NEG)
        expo = jnp.exp(logit - jnp.max(logit, axis=1, keepdims=True))
        share = expo / jnp.sum(expo, axis=1, keepdims=True)
        out[s] = LOSS * (share - mass * (1.0 / H))


def divergence(meta, pieces, samples, listed, n_ctx, after):
    rows, keys = pieces[0].shape
    return pl.pallas_call(
        functools.partial(divergence_kernel, samples, listed, n_ctx),
        out_shape=jax.ShapeDtypeStruct((samples, rows // samples // 2, keys), F32),
        in_specs=[smem_spec()] + [vmem_spec()] * n_ctx + [any_spec()] * len(after),
        out_specs=vmem_spec(),
        compiler_params=params(),
        cost_estimate=cost(0, n_ctx * rows * keys * 4),
        name="divergence",
    )(meta, *pieces, *after)


def indexer_kernel(dims, n_ctx, groups, extra, meta, *refs):
    samples, listed, slots, per_shard, width, tiles = dims
    near = 2 * n_ctx - 1
    iq_ref, wcol_ref = refs[:2]
    ikeys = refs[2 : 2 + samples]
    grads = refs[2 + samples : 2 + samples + n_ctx]
    refs = refs[2 + samples + n_ctx + extra :]
    diq_ref, dw_ref = refs[:2]
    outs = refs[2 : 2 + near]
    whole, ik_scr, acc_t, acc = refs[2 + near :]
    s, c = pl.program_id(0), pl.program_id(1)
    me = meta[samples * (listed + 1)]
    part, keys = grads[0].shape[1:]

    @pl.when(c == 0)
    def _():
        for k in range(n_ctx):
            whole[lax.rem(me - k + n_ctx, n_ctx)] = grads[k][s]
        for at in range(samples):

            @pl.when(s == at)
            def _(at=at):
                ik_scr[...] = ikeys[at][...]

        acc_t[...] = jnp.zeros_like(acc_t)

    iq = iq_ref[...]
    inner = lax.dot_general(iq, ik_scr[...], NT, preferred_element_type=F32)
    grad = whole[c]
    if groups % 8 == 0:
        grad = jnp.broadcast_to(grad[:, None, :], (part, groups, keys)).reshape(part * groups, keys)
    else:
        expand = (
            lax.broadcasted_iota(jnp.int32, (part * groups, part), 0) // groups
            == lax.broadcasted_iota(jnp.int32, (part * groups, part), 1)
        ).astype(F32)
        grad = jnp.dot(expand, grad, precision=EXACT, preferred_element_type=F32)
    edge = jnp.where(inner > 0.0, grad * (wcol_ref[...] * IDX_SCALE), 0.0).astype(BF16)
    dw_ref[...] = jnp.sum(grad * jnp.maximum(inner, 0.0), axis=1, keepdims=True) * IDX_SCALE
    diq_ref[...] = jnp.dot(edge, ik_scr[...], preferred_element_type=F32).astype(BF16)
    acc_t[...] += jnp.dot(iq.T, edge, preferred_element_type=F32)

    @pl.when(c == n_ctx - 1)
    def _():
        acc[...] = acc_t[...].T.astype(BF16)
        number = meta[samples * listed + s]
        for at in range(near):
            shard = shard_of(at, me, n_ctx)
            first, many = span(meta, s * listed, listed, number, shard, per_shard)

            def emit(j, _, out=outs[at], first=first):
                out[pl.ds(pl.multiple_of(j * BLK, BLK), BLK), :] = acc[
                    pl.ds(pl.multiple_of((first + j) * BLK, BLK), BLK), :
                ]
                return 0

            lax.fori_loop(0, many, emit, 0)


def indexer(meta, idx_query, wcol, ikeys, grads, dims, n_ctx, after):
    samples, listed, slots, per_shard, width, tiles = dims
    total, ind = idx_query.shape[1:]
    part, keys = grads[0].shape[1:]
    groups = total // (part * n_ctx)
    near = 2 * n_ctx - 1
    chunk = part * groups

    def rows(columns):
        return pl.BlockSpec((None, chunk, columns), lambda s, c: (s, c, 0))

    def whole(shape):
        return pl.BlockSpec(shape, lambda s, c: (0,) * len(shape))

    slot_rows = slots * BLK
    out = pl.pallas_call(
        functools.partial(indexer_kernel, dims, n_ctx, groups, len(after)),
        grid=(samples, n_ctx),
        out_shape=[
            jax.ShapeDtypeStruct(idx_query.shape, BF16),
            jax.ShapeDtypeStruct((samples, total, 1), F32),
        ]
        + [jax.ShapeDtypeStruct((samples, slot_rows, ind), BF16)] * near,
        in_specs=[smem_spec(), rows(ind), rows(1)]
        + [whole((keys, ind))] * samples
        + [whole(grads[0].shape)] * n_ctx
        + [any_spec()] * len(after),
        out_specs=[rows(ind), rows(1)]
        + [pl.BlockSpec((None, slot_rows, ind), lambda s, c: (s, 0, 0))] * near,
        scratch_shapes=[
            pltpu.VMEM((n_ctx, part, keys), F32),
            pltpu.VMEM((keys, ind), BF16),
            pltpu.VMEM((ind, keys), F32),
            pltpu.VMEM((keys, ind), BF16),
        ],
        compiler_params=params(),
        cost_estimate=cost(6 * samples * total * keys * ind, 8 * samples * total * LANE * 2),
        name="indexer",
    )(meta, idx_query, wcol, *ikeys, *grads, *after)
    return out[0], out[1], out[2:]


def settle_kernel(dims, n_smp, here, *refs):
    samples, listed, slots, per_shard, width, tiles = dims
    slabs = refs[: n_smp * samples]
    lasts = refs[n_smp * samples : n_smp * (samples + 1)]
    out_kv, out_ik, acc, acc_i = refs[n_smp * (samples + 1) :]
    each = samples * (listed + 1)
    me = here[n_smp * each]
    place = here[n_smp * each + 1]
    mine = per_shard // n_smp
    base = me * per_shard + place * mine
    value = tiles * LANE
    acc[...] = jnp.zeros_like(acc)
    acc_i[...] = jnp.zeros_like(acc_i)
    for at in range(n_smp):
        for s in range(samples):
            start = at * each + s * listed
            number = here[at * each + samples * listed + s]
            shard_first, _ = span(here, start, listed, number, me, per_shard)
            first = below(here, start, listed, number, base)
            last = below(here, start, listed, number, base + mine)

            skip = s * slots * BLK

            def add(
                i, _, slab=slabs[at * samples + s], ik=lasts[at], skip=skip, start=start,
                zero=shard_first,
            ):
                j = i - zero
                to = pl.multiple_of((here[start + i] - base) * BLK, BLK)
                rows = pl.ds(to, BLK)
                for c in range(tiles):
                    acc[rows, c * LANE : (c + 1) * LANE] += slab[
                        pl.ds(pl.multiple_of((c * slots + j) * BLK, BLK), BLK), :
                    ].astype(F32)
                tail = slab[
                    pl.ds(pl.multiple_of(tiles * slots * BLK + j * HALF, HALF), HALF), :
                ].astype(F32)
                side = LANE // 2
                acc[pl.ds(to, HALF), value : value + side] += tail[:, :side]
                acc[pl.ds(pl.multiple_of(to + HALF, HALF), HALF), value : value + side] += tail[
                    :, side:
                ]
                acc_i[rows, :] += ik[pl.ds(pl.multiple_of(skip + j * BLK, BLK), BLK), :].astype(F32)
                return 0

            lax.fori_loop(first, last, add, 0)
    for c in range(acc.shape[0] // LANE):
        rows = slice(c * LANE, (c + 1) * LANE)
        out_kv[:, rows] = acc[rows, :].astype(BF16).T[:width]
    out_ik[...] = acc_i[...].astype(BF16)


def settle(here, slabs, lasts, dims, n_smp):
    samples, listed, slots, per_shard, width, tiles = dims
    rows = per_shard * BLK // n_smp
    ind = lasts[0].shape[1]
    wide = (width + LANE - 1) // LANE * LANE
    return pl.pallas_call(
        functools.partial(settle_kernel, dims, n_smp),
        out_shape=[
            jax.ShapeDtypeStruct((width, rows), BF16),
            jax.ShapeDtypeStruct((rows, ind), BF16),
        ],
        in_specs=[smem_spec()] + [vmem_spec()] * (len(slabs) + len(lasts)),
        out_specs=[vmem_spec()] * 2,
        scratch_shapes=[pltpu.VMEM((rows, wide), F32), pltpu.VMEM((rows, ind), F32)],
        compiler_params=params(),
        cost_estimate=cost(0, 4 * rows * width * 2),
        name="settle",
    )(here, *slabs, *lasts)


def spread_blocks(own, n, holds=()):
    rights, lefts = [], []
    right = left = own
    for step in range(1, n):
        hold = holds[step - 1] if step <= len(holds) else []
        if hold and step == 1:
            right = left = tie([own], hold)[0]
        elif hold:
            right, left = tie([right, left], hold)
        right = lax.ppermute(right, "ctx", [(i, i + 1) for i in range(step - 1, n - 1)])
        left = lax.ppermute(left, "ctx", [(i, i - 1) for i in range(1, n - step + 1)])
        rights.append(right)
        lefts.append(left)
    return [own] + rights + lefts


def add(a, b):
    return (a.astype(F32) + b.astype(F32)).astype(BF16)


class Sums:
    def __init__(self, parts, n):
        self.own, self.before, self.later, self.n = parts[0], parts[1:n], parts[n:], n
        self.came = []

    def step(self, hold=()):
        far = self.n - 1 - len(self.came)
        left, right = self.before[far - 1], self.later[far - 1]
        if self.came:
            right, left = add(self.came[-1][0], right), add(self.came[-1][1], left)
        if hold:
            left, right = tie([left, right], list(hold))
        right = lax.ppermute(right, "ctx", [(i, i + 1) for i in range(self.n - far)])
        left = lax.ppermute(left, "ctx", [(i, i - 1) for i in range(far, self.n)])
        self.came.append([right, left])
        return self.came[-1]

    def total(self):
        right, left = self.came[-1]
        return (self.own.astype(F32) + right.astype(F32) + left.astype(F32)).astype(BF16)


def tie_kernel(*refs):
    pass


def tie(arrays, after):
    count = len(arrays)
    return list(
        pl.pallas_call(
            tie_kernel,
            out_shape=[jax.ShapeDtypeStruct(x.shape, x.dtype) for x in arrays],
            in_specs=[any_spec()] * (count + len(after)),
            out_specs=[any_spec()] * count,
            input_output_aliases={i: i for i in range(count)},
            compiler_params=params(),
            cost_estimate=cost(0, 0),
            name="tie",
        )(*arrays, *after)
    )


def shifted(x, axis, n, by):
    return lax.ppermute(x, axis, [(i, (i + by) % n) for i in range(n)])


def exchange(x, n):
    chips = [x] + [shifted(x, "smp", n, 2 * k) for k in range(1, n // 2)]
    other = [lax.ppermute(y, "smp", [(i, i ^ 1) for i in range(n)]) for y in chips]
    return chips + other


def shards(kv, idx_key, query, dout, idx_query, idx_weight, blocks, counts):
    n_ctx = lax.axis_size("ctx")
    n_smp = lax.axis_size("smp")
    me = lax.axis_index("ctx").astype(jnp.int32)
    place = lax.axis_index("smp").astype(jnp.int32)
    samples, listed = blocks.shape
    width = kv.shape[1]
    value = dout.shape[3]
    _, every, heads, _ = query.shape
    groups = idx_query.shape[2]
    dims = (
        samples,
        listed,
        max(2, 2 * listed // n_ctx),
        kv.shape[0] // BLK,
        width,
        value // LANE,
    )
    lists = jnp.concatenate([blocks.reshape(-1), counts])
    meta = jnp.concatenate([lists, me[None]])
    here = jnp.concatenate(exchange(lists, n_smp) + [jnp.stack([me, place])])
    q = query.reshape(samples, every * heads, width)
    do = dout.reshape(samples, every * heads, value)
    iq = idx_query.reshape(samples, every * groups, idx_query.shape[3])
    wcol = idx_weight.astype(F32).reshape(samples, every * groups, 1)
    tall = min(512, every * heads)
    steps = every * heads // tall

    packed = pack(meta, kv.T, idx_key, dims)
    slabs = [spread_blocks(packed[0], n_ctx)]
    d_query = None
    ikeys, parts, rings = [], [], []
    for s in range(samples):
        more = s + 1 < samples
        cut = steps // 2 if samples > 1 and steps > 1 else 0
        state, carry, ready = [], [], rings[-1].came[0] if rings else []
        if cut:
            d_query, state = attention(
                meta, q, do, iq, wcol, slabs[s], [], [], d_query, dims, s, n_ctx, heads, tall,
                0, cut, ready,
            )
            carry, ready = state[:1], []
        if more:
            before = slabs[s]
            coming = spread_blocks(
                packed[s + 1], n_ctx, [[before[n_ctx - 1], before[-1], here], state[:1]]
            )
            ring = [[coming[k], coming[k + n_ctx - 1]] for k in range(1, n_ctx)]
            slabs.append(coming)
            ready = ring[0]
        elif cut:
            ready = rings[0].came[1 % len(rings[0].came)]
        d_query, grads, parts, ikey = attention(
            meta, q, do, iq, wcol, slabs[s], state, parts, d_query, dims, s, n_ctx, heads, tall,
            cut, steps, ready,
        )
        ikeys.append(ikey)
        rings.append(Sums(grads, n_ctx))
        if more:
            rings[-1].step(ring[1 % len(ring)])
            if n_ctx > 2:
                rings[-1].step()
    last = rings[-1]
    for ring in rings[:-1]:
        while len(ring.came) < n_ctx - 1:
            ring.step(carry)
    last.step(rings[0].came[-1] if samples > 1 else [])
    pieces = [parts[0]] + [shifted(parts[k], "ctx", n_ctx, k) for k in range(1, n_ctx)]
    grad = divergence(meta, pieces, samples, listed, n_ctx, last.came[0])
    grads = [grad] + [shifted(grad, "ctx", n_ctx, k) for k in range(1, n_ctx)]
    last.step([grad])
    exchanged = []
    for ring in rings[:-1]:
        exchanged.append(exchange(ring.total(), n_smp))
    d_idx_query, d_weight, parts = indexer(meta, iq, wcol, ikeys, grads, dims, n_ctx, [])
    small = Sums([x.reshape(-1, x.shape[-1]) for x in parts], n_ctx)
    small.step(last.came[-1])
    hold = [y for x in exchanged for y in x[1 : n_smp // 2]]
    while len(last.came) < n_ctx - 1:
        last.step()
        small.step(last.came[-1] + hold)
        hold = []
    small.step(hold)
    total = exchange(last.total(), n_smp)
    exchanged.append(total)
    out_kv, out_ik = settle(
        here,
        [exchanged[s][at] for at in range(n_smp) for s in range(samples)],
        exchange(small.total(), n_smp),
        dims,
        n_smp,
    )
    return (
        d_query.reshape(query.shape),
        d_idx_query.reshape(idx_query.shape),
        d_weight.reshape(idx_weight.shape).astype(BF16),
        out_kv.T,
        out_ik,
    )


def solution(mesh):
    return jax.shard_map(
        shards,
        mesh=mesh,
        in_specs=(
            P(("rep", "ctx"), None),
            P(("rep", "ctx"), None),
            P(("rep", "smp"), None, "ctx", None),
            P(("rep", "smp"), None, "ctx", None),
            P(("rep", "smp"), None, "ctx", None),
            P(("rep", "smp"), None, "ctx"),
            P(("rep", "smp"), None),
            P(("rep", "smp")),
        ),
        out_specs=(
            P(("rep", "smp"), None, "ctx", None),
            P(("rep", "smp"), None, "ctx", None),
            P(("rep", "smp"), None, "ctx"),
            P(("rep", "ctx", "smp"), None),
            P(("rep", "ctx", "smp"), None),
        ),
        check_vma=False,
    )
```

time: 379 us -> 299 us (0.79)
  waiting for transfers between devices: 144 us -> 90.6 us
  starting transfers between devices: 106 us -> 81.5 us
  blocking collectives: 7.03 us -> 0 us
  other arithmetic: 5.89 us -> 12.2 us
  local copies, waits for them, and re-layouts: 24.6 us -> 18.5 us
    ppermute x18, waiting for transfers between devices: 43.9 us -> 18.9 us  [the longest x9 14.6 us: step(): lax.ppermute(right, 'ctx', [(i, i + 1) for i in range(self.n - far)])]
    ppermute x12 -> x10, starting transfers between devices: 38.9 us -> 14.9 us  [shifted(): return lax.ppermute(x, axis, [(i, (i + by) % n) for i in range(n)])]
    ppermute x6, waiting for transfers between devices: 58.5 us -> 43.1 us  [spread_blocks(): lax.ppermute(left, 'ctx', [(i, i - 1) for i in range(1, n - step + 1)])]
    ppermute x12 -> x10, waiting for transfers between devices: 40.9 us -> 28.2 us  [shifted(): return lax.ppermute(x, axis, [(i, (i + by) % n) for i in range(n)])]
    unnamed x1 -> x0, blocking collectives: 7.03 us -> none
    unnamed x93 -> x132, local copies, waits for them, and re-layouts: 22.1 us -> 15.3 us
    convert_element_type x12, other arithmetic: 3.5 us -> 8.53 us  [add(): return (a.astype(F32) + b.astype(F32)).astype(BF16)]
    pallas_call x2 -> x4, Pallas kernels: 66 us -> 66.8 us  [attention(): pl.pallas_call(functools.partial(attention_kernel, dims, s, n_ctx, heads,...]
  transfers between devices with their start and end apart: 48 -> 48, of which waited for: 22 -> 16; matrix products, arithmetic and copies ran while one was open for 2% -> 5% of each run, Pallas kernels for 9% -> 26%
where the time goes in v2:
time: 299 us; the launch traced here: 296 us
  Pallas kernels  91.3 us (31%)
  waiting for transfers between devices  90.6 us (30%)
  starting transfers between devices  81.5 us (27%)
  local copies, waits for them, and re-layouts  18.5 us (6%)
  other arithmetic  12.2 us (4%)
    pallas_call x4, Pallas kernels, attention(): pl.pallas_call(functools.partial(attention_kernel, dims, s, n_ctx, heads,...  66.8 us
    ppermute x6, waiting for transfers between devices, spread_blocks(): lax.ppermute(left, 'ctx', [(i, i - 1) for i in range(1, n - step + 1)])  43.1 us
    ppermute x9, starting transfers between devices, step(): lax.ppermute(right, 'ctx', [(i, i + 1) for i in range(self.n - far)])  34.7 us
    ppermute x10, waiting for transfers between devices, shifted(): return lax.ppermute(x, axis, [(i, (i + by) % n) for i in range(n)])  28.2 us
    unnamed x132, local copies, waits for them, and re-layouts  15.3 us
    ppermute x10, starting transfers between devices, shifted(): return lax.ppermute(x, axis, [(i, (i + by) % n) for i in range(n)])  14.9 us
    ppermute x9, waiting for transfers between devices, step(): lax.ppermute(right, 'ctx', [(i, i + 1) for i in range(self.n - far)])  14.6 us
    ppermute x6, starting transfers between devices, spread_blocks(): lax.ppermute(right, 'ctx', [(i, i + 1) for i in range(step - 1, n - 1)])  14.2 us
  transfers between devices with their start and end apart: 48, of which 16 were waited for; matrix products, arithmetic and copies ran while one was open for 5% of the time, Pallas kernels for 26%

profile of v2, /device:TPU:0, one launch (start us, length us, event | category | flops | bytes accessed | tf_op | source)
XLA Modules:
  0.0 295.6 jit_solution(14969102193114523562)
XLA Ops:
  2.7 5.8 %pack.1 = (bf16[2816,128]{1,0:T(8,128)(2,1)}, bf16[2816,128]{1,0:T(8,128)(2,1)}) custom-call(s32[35]{0:T(128)} %pad_add_fusion.meta, bf16[576,8192]{1,0:T(8,128)(2,1)} %bitcast.35, bf16[8192,128]{1,0:T(8,128)(2,1)} %ik.1), custom_call_target="tpu_custom_call" | custom-call | bytes 5767168 | tf_op jit(solution)/shard_map/pack/pallas_call | solution.py:98
  9.8 5.9 %collective-permute-start = (bf16[2816,128]{1,0:T(8,128)(2,1)}, bf16[2816,128]{1,0:T(8,128)(2,1)S(1)}, u32[]{:S(2)}, u32[]{:S(2)}) collective-permute-start(bf16[2816,128]{1,0:T(8,128)(2,1)} %get-tuple-element.71.refs_4_), channel_id=1, source_target_pairs={{0,4},{4,8},{8,12},{1,5},{5,9},{9,13},{2,6},{6,10},{10,14},{3,7},{... | collective-permute-start | bytes 2162696 | tf_op jit(solution)/shard_map/ppermute | solution.py:566
  15.7 14.4 %collective-permute-done.3.refs_8_ = bf16[2816,128]{1,0:T(8,128)(2,1)S(1)} collective-permute-done((bf16[2816,128]{1,0:T(8,128)(2,1)}, bf16[2816,128]{1,0:T(8,128)(2,1)S(1)}, u32[]{:S(2)}, u32[]{:S(2)}) %collective-permute-start.3) | collective-permute-done | bytes 720928 | tf_op jit(solution)/shard_map/ppermute | solution.py:567
  33.0 16.4 %collective-permute-done.4.refs_9_ = bf16[2816,128]{1,0:T(8,128)(2,1)} collective-permute-done((bf16[2816,128]{1,0:T(8,128)(2,1)S(1)}, bf16[2816,128]{1,0:T(8,128)(2,1)}, u32[]{:S(2)}, u32[]{:S(2)}) %collective-permute-start.4) | collective-permute-done | bytes 720928 | tf_op jit(solution)/shard_map/ppermute | solution.py:567
  57.9 10.0 %collective-permute-done.5.refs_2_.refs_10_ = bf16[2816,128]{1,0:T(8,128)(2,1)S(1)} collective-permute-done((bf16[2816,128]{1,0:T(8,128)(2,1)}, bf16[2816,128]{1,0:T(8,128)(2,1)S(1)}, u32[]{:S(2)}, u32[]{:S(2)}) %collective-permute-start.5) | collective-permute-done | bytes 720928 | tf_op jit(solution)/shard_map/ppermute | solution.py:567
  70.9 4.6 %collective-permute-start.9 = (bf16[2816,128]{1,0:T(8,128)(2,1)}, bf16[2816,128]{1,0:T(8,128)(2,1)S(1)}, u32[]{:S(2)}, u32[]{:S(2)}) collective-permute-start(bf16[2816,128]{1,0:T(8,128)(2,1)} %tie.8), channel_id=1, source_target_pairs={{0,4},{4,8},{8,12},{1,5},{5,9},{9,13},{2,6},{6,10},{10,14},{3,7},{... | collective-permute-start | bytes 2162696 | tf_op jit(solution)/shard_map/ppermute | solution.py:566
  77.2 16.4 %attention.4 = (bf16[2,2048,576]{2,1,0:T(8,128)(2,1)}, bf16[1024,128]{1,0:T(8,128)(2,1)}, bf16[1024,640]{1,0:T(8,128)(2,1)}, bf16[640,1024]{1,0:T(8,128)(2,1)}, ...) custom-call(s32[35]{0:T(128)} %pad_add_fusion.meta, bf16[2,2048,576]{2,1,0:T(8,128)(2,1)} %bitcast.26, ...), custom_call_target="tpu_custom_call" | custom-call | flops 5771362304 | bytes 11665408 | tf_op jit(solution)/shard_map/attention/pallas_call | solution.py:332
  97.9 17.2 %attention.5 = (bf16[2,2048,576]{2,1,0:T(8,128)(2,1)}, bf16[2304,128]{1,0:T(8,128)(2,1)}, bf16[2304,128]{1,0:T(8,128)(2,1)}, bf16[2304,128]{1,0:T(8,128)(2,1)}, ...) custom-call(s32[35]{0:T(128)} %pad_add_fusion.meta, ...), custom_call_target="tpu_custom_call", output_to_operand_aliasing={{0}: (11, {})} | custom-call | flops 5771362304 | bytes 11665408 | tf_op jit(solution)/shard_map/attention/pallas_call | solution.py:332
  116.2 6.4 %collective-permute-start.15 = (bf16[2304,128]{1,0:T(8,128)(2,1)}, bf16[2304,128]{1,0:T(8,128)(2,1)S(1)}, u32[]{:S(2)}, u32[]{:S(2)}) collective-permute-start(bf16[2304,128]{1,0:T(8,128)(2,1)} %get-tuple-element.84), channel_id=1, source_target_pairs={{0,4},{1,5},{2,6},{3,7},{16,20},{17,21},{18,22},{19,23}} | collective-permute-start | bytes 1769480 | tf_op jit(solution)/shard_map/ppermute | solution.py:589
  125.3 6.5 %collective-permute-done.15.refs_12_ = bf16[2304,128]{1,0:T(8,128)(2,1)S(1)} collective-permute-done((bf16[2304,128]{1,0:T(8,128)(2,1)}, bf16[2304,128]{1,0:T(8,128)(2,1)S(1)}, u32[]{:S(2)}, u32[]{:S(2)}) %collective-permute-start.15) | collective-permute-done | bytes 589856 | tf_op jit(solution)/shard_map/ppermute | solution.py:589
  132.0 4.3 %collective-permute-start.17 = (bf16[2304,128]{1,0:T(8,128)(2,1)S(1)}, bf16[2304,128]{1,0:T(8,128)(2,1)S(1)}, u32[]{:S(2)}, u32[]{:S(2)}) collective-permute-start(bf16[2304,128]{1,0:T(8,128)(2,1)S(1)} %add_convert_fusion.9), channel_id=1, source_target_pairs={{0,4},{4,8},{1,5},{5,9},{2,6},{6,10},{3,7},{7,11},{16,20},{20,24},... | collective-permute-start | bytes 1769480 | tf_op jit(solution)/shard_map/ppermute | solution.py:589
  140.4 16.1 %attention.6 = (bf16[2,2048,576]{2,1,0:T(8,128)(2,1)}, bf16[1024,128]{1,0:T(8,128)(2,1)}, bf16[1024,640]{1,0:T(8,128)(2,1)}, bf16[640,1024]{1,0:T(8,128)(2,1)}, ...) custom-call(s32[35]{0:T(128)} %pad_add_fusion.meta, ...), custom_call_target="tpu_custom_call", output_to_operand_aliasing={{0}: (12, {})} | custom-call | flops 5771362304 | bytes 11665408 | tf_op jit(solution)/shard_map/attention/pallas_call | solution.py:332
  162.0 17.1 %attention.7 = (bf16[2,2048,576]{2,1,0:T(8,128)(2,1)}, bf16[2304,128]{1,0:T(8,128)(2,1)}, bf16[2304,128]{1,0:T(8,128)(2,1)}, bf16[2304,128]{1,0:T(8,128)(2,1)}, ...) custom-call(s32[35]{0:T(128)} %pad_add_fusion.meta, ...), custom_call_target="tpu_custom_call", output_to_operand_aliasing={{0}: (15, {})} | custom-call | flops 5771362304 | bytes 11665408 | tf_op jit(solution)/shard_map/attention/pallas_call | solution.py:332
  180.1 4.7 %collective-permute-start.24 = (bf16[2304,128]{1,0:T(8,128)(2,1)}, bf16[2304,128]{1,0:T(8,128)(2,1)S(1)}, u32[]{:S(2)}, u32[]{:S(2)}) collective-permute-start(bf16[2304,128]{1,0:T(8,128)(2,1)} %get-tuple-element.110), channel_id=1, source_target_pairs={{0,4},{1,5},{2,6},{3,7},{16,20},{17,21},{18,22},{19,23}} | collective-permute-start | bytes 1769480 | tf_op jit(solution)/shard_map/ppermute | solution.py:589
  189.5 16.9 %collective-permute-done.19.refs_1_ = f32[64,1024]{1,0:T(8,128)S(1)} collective-permute-done((f32[64,1024]{1,0:T(8,128)S(1)}, f32[64,1024]{1,0:T(8,128)S(1)}, u32[]{:S(2)}, u32[]{:S(2)}) %collective-permute-start.19) | collective-permute-done | bytes 262176 | tf_op jit(solution)/shard_map/ppermute | solution.py:620
  211.6 4.5 %collective-permute-start.28 = (f32[2,16,1024]{2,1,0:T(8,128)}, f32[2,16,1024]{2,1,0:T(8,128)S(1)}, u32[]{:S(2)}, u32[]{:S(2)}) collective-permute-start(f32[2,16,1024]{2,1,0:T(8,128)} %divergence.1.refs_4_.refs_2_), channel_id=1, source_target_pairs={{0,12},{4,0},{8,4},{12,8},{1,13},{5,1},{9,5},{13,9},{2,14},{6,2},{... | collective-permute-start | bytes 393224 | tf_op jit(solution)/shard_map/ppermute | solution.py:620
  229.4 10.1 %indexer.1 = (bf16[2,1024,128]{2,1,0:T(8,128)(2,1)}, f32[2,1024,1]{2,1,0:T(8,128)}, bf16[2,512,128]{2,1,0:T(8,128)(2,1)}, bf16[2,512,128]{2,1,0:T(8,128)(2,1)}, ...) custom-call(s32[35]{0:T(128)} %pad_add_fusion.meta, ...), custom_call_target="tpu_custom_call" | custom-call | flops 1610612736 | bytes 4194304 | tf_op jit(solution)/shard_map/indexer/pallas_call | solution.py:458
  245.6 4.8 %collective-permute-start.40 = (bf16[1024,128]{1,0:T(8,128)(2,1)S(1)}, bf16[1024,128]{1,0:T(8,128)(2,1)S(1)}, u32[]{:S(2)}, u32[]{:S(2)}) collective-permute-start(bf16[1024,128]{1,0:T(8,128)(2,1)S(1)} %copy-done.53), channel_id=1, source_target_pairs={{0,4},{1,5},{2,6},{3,7},{16,20},{17,21},{18,22},{19,23}} | collective-permute-start | bytes 786440 | tf_op jit(solution)/shard_map/ppermute | solution.py:589
  251.2 4.0 %collective-permute-done.40 = bf16[1024,128]{1,0:T(8,128)(2,1)S(1)} collective-permute-done((bf16[1024,128]{1,0:T(8,128)(2,1)S(1)}, bf16[1024,128]{1,0:T(8,128)(2,1)S(1)}, u32[]{:S(2)}, u32[]{:S(2)}) %collective-permute-start.40) | collective-permute-done | bytes 262176 | tf_op jit(solution)/shard_map/ppermute | solution.py:589
  257.8 4.4 %collective-permute-start.41 = (bf16[1024,128]{1,0:T(8,128)(2,1)}, bf16[1024,128]{1,0:T(8,128)(2,1)S(1)}, u32[]{:S(2)}, u32[]{:S(2)}) collective-permute-start(bf16[1024,128]{1,0:T(8,128)(2,1)} %get-tuple-element.129), channel_id=1, source_target_pairs={{0,4},{4,8},{1,5},{5,9},{2,6},{6,10},{3,7},{7,11},{16,20},{20,24},... | collective-permute-start | bytes 786440 | tf_op jit(solution)/shard_map/ppermute | solution.py:589
  267.4 4.4 %collective-permute-start.42 = (bf16[1024,128]{1,0:T(8,128)(2,1)S(1)}, bf16[1024,128]{1,0:T(8,128)(2,1)S(1)}, u32[]{:S(2)}, u32[]{:S(2)}) collective-permute-start(bf16[1024,128]{1,0:T(8,128)(2,1)S(1)} %fusion.1), channel_id=1, source_target_pairs={{0,4},{4,8},{8,12},{1,5},{5,9},{9,13},{2,6},{6,10},{10,14},{3,7},{... | collective-permute-start | bytes 786440 | tf_op jit(solution)/shard_map/ppermute | solution.py:589
  276.2 4.0 %collective-permute-done.44 = bf16[1024,128]{1,0:T(8,128)(2,1)S(1)} collective-permute-done((bf16[1024,128]{1,0:T(8,128)(2,1)S(1)}, bf16[1024,128]{1,0:T(8,128)(2,1)S(1)}, u32[]{:S(2)}, u32[]{:S(2)}) %collective-permute-start.44) | collective-permute-done | bytes 262176 | tf_op jit(solution)/shard_map/ppermute | solution.py:590
  282.2 4.6 %collective-permute-done.45.refs_9_ = bf16[1024,128]{1,0:T(8,128)(2,1)S(1)} collective-permute-done((bf16[1024,128]{1,0:T(8,128)(2,1)S(1)}, bf16[1024,128]{1,0:T(8,128)(2,1)S(1)}, u32[]{:S(2)}, u32[]{:S(2)}) %collective-permute-start.45) | collective-permute-done | bytes 262176 | tf_op jit(solution)/shard_map/ppermute | solution.py:620
  289.0 6.6 %settle.1 = (bf16[576,2048]{1,0:T(8,128)(2,1)}, bf16[2048,128]{1,0:T(8,128)(2,1)}) custom-call(s32[138]{0:T(256)} %concatenate.13.refs_3_.here, bf16[2304,128]{1,0:T(8,128)(2,1)} %copy-done.8, bf16[2304,128]{1,0:T(8,128)(2,1)} %copy-done.9, bf16[2304,128]{1,0:T(8,128)(2,1)} %copy-done.4, bf16[2304,128]{1,0:T(8,128)(2,1)} %copy-done.30, ...), custom_call_target="tpu_custom_call" | custom-call | bytes 9437184 | tf_op jit(solution)/shard_map/settle/pallas_call | solution.py:542
  (243 shorter events, 83.9 us)
Async XLA Ops:
  8.5 21.6 %collective-permute-start.3 = (bf16[2816,128]{1,0:T(8,128)(2,1)}, bf16[2816,128]{1,0:T(8,128)(2,1)S(1)}, u32[]{:S(2)}, u32[]{:S(2)}) collective-permute-start(bf16[2816,128]{1,0:T(8,128)(2,1)} %get-tuple-element.71.refs_4_), channel_id=1, source_target_pairs={{4,0},{8,4},{12,8},{5,1},{9,5},{13,9},{6,2},{10,6},{14,10},{7,3},{... | collective-permute-start | bytes 2162696 | tf_op jit(solution)/shard_map/ppermute | solution.py:567
  9.8 21.6 %collective-permute-start = (bf16[2816,128]{1,0:T(8,128)(2,1)}, bf16[2816,128]{1,0:T(8,128)(2,1)S(1)}, u32[]{:S(2)}, u32[]{:S(2)}) collective-permute-start(bf16[2816,128]{1,0:T(8,128)(2,1)} %get-tuple-element.71.refs_4_), channel_id=1, source_target_pairs={{0,4},{4,8},{8,12},{1,5},{5,9},{9,13},{2,6},{6,10},{10,14},{3,7},{... | collective-permute-start | bytes 2162696 | tf_op jit(solution)/shard_map/ppermute | solution.py:566
  30.1 19.3 %collective-permute-start.4 = (bf16[2816,128]{1,0:T(8,128)(2,1)S(1)}, bf16[2816,128]{1,0:T(8,128)(2,1)}, u32[]{:S(2)}, u32[]{:S(2)}) collective-permute-start(bf16[2816,128]{1,0:T(8,128)(2,1)S(1)} %collective-permute-done.3.refs_8_), channel_id=1, source_target_pairs={{4,0},{8,4},{5,1},{9,5},{6,2},{10,6},{7,3},{11,7},{20,16},{24,20},... | collective-permute-start | bytes 2162696 | tf_op jit(solution)/shard_map/ppermute | solution.py:567
  31.4 19.3 %collective-permute-start.1 = (bf16[2816,128]{1,0:T(8,128)(2,1)S(1)}, bf16[2816,128]{1,0:T(8,128)(2,1)}, u32[]{:S(2)}, u32[]{:S(2)}) collective-permute-start(bf16[2816,128]{1,0:T(8,128)(2,1)S(1)} %collective-permute-done.refs_5_), channel_id=1, source_target_pairs={{4,8},{8,12},{5,9},{9,13},{6,10},{10,14},{7,11},{11,15},{20,24},{2... | collective-permute-start | bytes 2162696 | tf_op jit(solution)/shard_map/ppermute | solution.py:566
  49.4 18.5 %collective-permute-start.5 = (bf16[2816,128]{1,0:T(8,128)(2,1)}, bf16[2816,128]{1,0:T(8,128)(2,1)S(1)}, u32[]{:S(2)}, u32[]{:S(2)}) collective-permute-start(bf16[2816,128]{1,0:T(8,128)(2,1)} %collective-permute-done.4.refs_9_), channel_id=1, source_target_pairs={{4,0},{5,1},{6,2},{7,3},{20,16},{21,17},{22,18},{23,19}} | collective-permute-start | bytes 2162696 | tf_op jit(solution)/shard_map/ppermute | solution.py:567
  50.7 17.2 %collective-permute-start.2 = (bf16[2816,128]{1,0:T(8,128)(2,1)}, bf16[2816,128]{1,0:T(8,128)(2,1)S(1)}, u32[]{:S(2)}, u32[]{:S(2)}) collective-permute-start(bf16[2816,128]{1,0:T(8,128)(2,1)} %collective-permute-done.1.refs_6_), channel_id=1, source_target_pairs={{8,12},{9,13},{10,14},{11,15},{24,28},{25,29},{26,30},{27,31}} | collective-permute-start | bytes 2162696 | tf_op jit(solution)/shard_map/ppermute | solution.py:566
  69.6 24.0 %collective-permute-start.10 = (bf16[2816,128]{1,0:T(8,128)(2,1)}, bf16[2816,128]{1,0:T(8,128)(2,1)S(1)}, u32[]{:S(2)}, u32[]{:S(2)}) collective-permute-start(bf16[2816,128]{1,0:T(8,128)(2,1)} %tie.8), channel_id=1, source_target_pairs={{4,0},{8,4},{12,8},{5,1},{9,5},{13,9},{6,2},{10,6},{14,10},{7,3},{... | collective-permute-start | bytes 2162696 | tf_op jit(solution)/shard_map/ppermute | solution.py:567
  70.9 23.6 %collective-permute-start.9 = (bf16[2816,128]{1,0:T(8,128)(2,1)}, bf16[2816,128]{1,0:T(8,128)(2,1)S(1)}, u32[]{:S(2)}, u32[]{:S(2)}) collective-permute-start(bf16[2816,128]{1,0:T(8,128)(2,1)} %tie.8), channel_id=1, source_target_pairs={{0,4},{4,8},{8,12},{1,5},{5,9},{9,13},{2,6},{6,10},{10,14},{3,7},{... | collective-permute-start | bytes 2162696 | tf_op jit(solution)/shard_map/ppermute | solution.py:566
  95.7 19.4 %collective-permute-start.11 = (bf16[2816,128]{1,0:T(8,128)(2,1)}, bf16[2816,128]{1,0:T(8,128)(2,1)S(1)}, u32[]{:S(2)}, u32[]{:S(2)}) collective-permute-start(bf16[2816,128]{1,0:T(8,128)(2,1)} %get-tuple-element.73), channel_id=1, source_target_pairs={{4,8},{8,12},{5,9},{9,13},{6,10},{10,14},{7,11},{11,15},{20,24},{2... | collective-permute-start | bytes 2162696 | tf_op jit(solution)/shard_map/ppermute | solution.py:566
  96.4 18.7 %collective-permute-start.13 = (bf16[2816,128]{1,0:T(8,128)(2,1)}, bf16[2816,128]{1,0:T(8,128)(2,1)S(1)}, u32[]{:S(2)}, u32[]{:S(2)}) collective-permute-start(bf16[2816,128]{1,0:T(8,128)(2,1)} %get-tuple-element.74), channel_id=1, source_target_pairs={{4,0},{8,4},{5,1},{9,5},{6,2},{10,6},{7,3},{11,7},{20,16},{24,20},... | collective-permute-start | bytes 2162696 | tf_op jit(solution)/shard_map/ppermute | solution.py:567
  116.2 15.6 %collective-permute-start.15 = (bf16[2304,128]{1,0:T(8,128)(2,1)}, bf16[2304,128]{1,0:T(8,128)(2,1)S(1)}, u32[]{:S(2)}, u32[]{:S(2)}) collective-permute-start(bf16[2304,128]{1,0:T(8,128)(2,1)} %get-tuple-element.84), channel_id=1, source_target_pairs={{0,4},{1,5},{2,6},{3,7},{16,20},{17,21},{18,22},{19,23}} | collective-permute-start | bytes 1769480 | tf_op jit(solution)/shard_map/ppermute | solution.py:589
  132.0 24.5 %collective-permute-start.17 = (bf16[2304,128]{1,0:T(8,128)(2,1)S(1)}, bf16[2304,128]{1,0:T(8,128)(2,1)S(1)}, u32[]{:S(2)}, u32[]{:S(2)}) collective-permute-start(bf16[2304,128]{1,0:T(8,128)(2,1)S(1)} %add_convert_fusion.9), channel_id=1, source_target_pairs={{0,4},{4,8},{1,5},{5,9},{2,6},{6,10},{3,7},{7,11},{16,20},{20,24},... | collective-permute-start | bytes 1769480 | tf_op jit(solution)/shard_map/ppermute | solution.py:589
  136.5 21.0 %collective-permute-start.18 = (bf16[2304,128]{1,0:T(8,128)(2,1)S(1)}, bf16[2304,128]{1,0:T(8,128)(2,1)S(1)}, u32[]{:S(2)}, u32[]{:S(2)}) collective-permute-start(bf16[2304,128]{1,0:T(8,128)(2,1)S(1)} %add_convert_fusion.8), channel_id=1, source_target_pairs={{8,4},{12,8},{9,5},{13,9},{10,6},{14,10},{11,7},{15,11},{24,20},{2... | collective-permute-start | bytes 1769480 | tf_op jit(solution)/shard_map/ppermute | solution.py:590
  158.9 20.2 %collective-permute-start.22 = (bf16[2304,128]{1,0:T(8,128)(2,1)}, bf16[2304,128]{1,0:T(8,128)(2,1)S(1)}, u32[]{:S(2)}, u32[]{:S(2)}) collective-permute-start(bf16[2304,128]{1,0:T(8,128)(2,1)} %get-tuple-element.108), channel_id=1, source_target_pairs={{0,4},{4,8},{8,12},{1,5},{5,9},{9,13},{2,6},{6,10},{10,14},{3,7},{... | collective-permute-start | bytes 1769480 | tf_op jit(solution)/shard_map/ppermute | solution.py:589
  160.5 18.6 %collective-permute-start.23 = (bf16[2304,128]{1,0:T(8,128)(2,1)}, bf16[2304,128]{1,0:T(8,128)(2,1)S(1)}, u32[]{:S(2)}, u32[]{:S(2)}) collective-permute-start(bf16[2304,128]{1,0:T(8,128)(2,1)} %get-tuple-element.109), channel_id=1, source_target_pairs={{4,0},{8,4},{12,8},{5,1},{9,5},{13,9},{6,2},{10,6},{14,10},{7,3},{... | collective-permute-start | bytes 1769480 | tf_op jit(solution)/shard_map/ppermute | solution.py:590
  180.1 28.3 %collective-permute-start.24 = (bf16[2304,128]{1,0:T(8,128)(2,1)}, bf16[2304,128]{1,0:T(8,128)(2,1)S(1)}, u32[]{:S(2)}, u32[]{:S(2)}) collective-permute-start(bf16[2304,128]{1,0:T(8,128)(2,1)} %get-tuple-element.110), channel_id=1, source_target_pairs={{0,4},{1,5},{2,6},{3,7},{16,20},{17,21},{18,22},{19,23}} | collective-permute-start | bytes 1769480 | tf_op jit(solution)/shard_map/ppermute | solution.py:589
  184.8 23.6 %collective-permute-start.25 = (bf16[2304,128]{1,0:T(8,128)(2,1)}, bf16[2304,128]{1,0:T(8,128)(2,1)S(1)}, u32[]{:S(2)}, u32[]{:S(2)}) collective-permute-start(bf16[2304,128]{1,0:T(8,128)(2,1)} %get-tuple-element.111), channel_id=1, source_target_pairs={{12,8},{13,9},{14,10},{15,11},{28,24},{29,25},{30,26},{31,27}} | collective-permute-start | bytes 1769480 | tf_op jit(solution)/shard_map/ppermute | solution.py:590
  185.5 20.9 %collective-permute-start.19 = (f32[64,1024]{1,0:T(8,128)S(1)}, f32[64,1024]{1,0:T(8,128)S(1)}, u32[]{:S(2)}, u32[]{:S(2)}) collective-permute-start(f32[64,1024]{1,0:T(8,128)S(1)} %copy-done.60), channel_id=1, source_target_pairs={{0,4},{4,8},{8,12},{12,0},{1,5},{5,9},{9,13},{13,1},{2,6},{6,10},{... | collective-permute-start | bytes 786440 | tf_op jit(solution)/shard_map/ppermute | solution.py:620
  185.6 20.8 %collective-permute-start.20 = (f32[64,1024]{1,0:T(8,128)S(1)}, f32[64,1024]{1,0:T(8,128)S(1)}, u32[]{:S(2)}, u32[]{:S(2)}) collective-permute-start(f32[64,1024]{1,0:T(8,128)S(1)} %copy-done.59), channel_id=1, source_target_pairs={{0,8},{4,12},{8,0},{12,4},{1,9},{5,13},{9,1},{13,5},{2,10},{6,14},... | collective-permute-start | bytes 786440 | tf_op jit(solution)/shard_map/ppermute | solution.py:620
  188.7 19.7 %collective-permute-start.21 = (f32[64,1024]{1,0:T(8,128)S(1)}, f32[64,1024]{1,0:T(8,128)S(1)}, u32[]{:S(2)}, u32[]{:S(2)}) collective-permute-start(f32[64,1024]{1,0:T(8,128)S(1)} %copy-done.58), channel_id=1, source_target_pairs={{0,12},{4,0},{8,4},{12,8},{1,13},{5,1},{9,5},{13,9},{2,14},{6,2},{... | collective-permute-start | bytes 786440 | tf_op jit(solution)/shard_map/ppermute | solution.py:620
  222.3 17.1 %collective-permute-start.29 = (bf16[2304,128]{1,0:T(8,128)(2,1)}, bf16[2304,128]{1,0:T(8,128)(2,1)S(1)}, u32[]{:S(2)}, u32[]{:S(2)}) collective-permute-start(bf16[2304,128]{1,0:T(8,128)(2,1)} %get-tuple-element.118), channel_id=1, source_target_pairs={{0,4},{4,8},{1,5},{5,9},{2,6},{6,10},{3,7},{7,11},{16,20},{20,24},... | collective-permute-start | bytes 1769480 | tf_op jit(solution)/shard_map/ppermute | solution.py:589
  224.9 31.1 %collective-permute-start.33 = (bf16[2304,128]{1,0:T(8,128)(2,1)S(1)}, bf16[2304,128]{1,0:T(8,128)(2,1)S(1)}, u32[]{:S(2)}, u32[]{:S(2)}) collective-permute-start(bf16[2304,128]{1,0:T(8,128)(2,1)S(1)} %add_convert_fusion.5.refs_0_), channel_id=1, source_target_pairs={{0,2},{1,3},{2,0},{3,1},{4,6},{5,7},{6,4},{7,5},{8,10},{9,11},{10,... | collective-permute-start | bytes 1769480 | tf_op jit(solution)/shard_map/ppermute | solution.py:620
  225.8 15.6 %collective-permute-start.31 = (bf16[2304,128]{1,0:T(8,128)(2,1)S(1)}, bf16[2304,128]{1,0:T(8,128)(2,1)S(1)}, u32[]{:S(2)}, u32[]{:S(2)}) collective-permute-start(bf16[2304,128]{1,0:T(8,128)(2,1)S(1)} %copy-done.15), channel_id=1, source_target_pairs={{8,4},{12,8},{9,5},{13,9},{10,6},{14,10},{11,7},{15,11},{24,20},{2... | collective-permute-start | bytes 1769480 | tf_op jit(solution)/shard_map/ppermute | solution.py:590
  239.6 16.4 %collective-permute-start.30 = (bf16[2304,128]{1,0:T(8,128)(2,1)S(1)}, bf16[2304,128]{1,0:T(8,128)(2,1)S(1)}, u32[]{:S(2)}, u32[]{:S(2)}) collective-permute-start(bf16[2304,128]{1,0:T(8,128)(2,1)S(1)} %add_convert_fusion.2), channel_id=1, source_target_pairs={{0,4},{4,8},{8,12},{1,5},{5,9},{9,13},{2,6},{6,10},{10,14},{3,7},{... | collective-permute-start | bytes 1769480 | tf_op jit(solution)/shard_map/ppermute | solution.py:589
  (88 other events, 727.2 us)
